TPU v7x, 512 devices: a whole 4x8x8 slice. The times are simulated.
512 devices in a mesh: clip: 16 (over z_hi, x), frame: 32 (over y, z_lo, core).
Axes of the slice: x: 4, y: 8, z: 8 (z_hi: 4, z_lo: 2; z = z_hi * 2 + z_lo), core: 2. Of those that a mesh axis runs over, the one named last changes fastest.
Arguments:
- queries: bfloat16 [16, 32, 256, 1152], P('clip', 'frame'), may hold values from -16 to 16
- keys: bfloat16 [16, 32, 256, 1152], P('clip', 'frame'), may hold values from -16 to 16
- values: bfloat16 [16, 32, 256, 1152], P('clip', 'frame'), may hold values from -6 to 6
- grad_out: bfloat16 [16, 32, 256, 1152], P('clip', 'frame'), may hold values from -6 to 6
- w_out: bfloat16 [1152, 1152], P('frame'), may hold values from -0.1875 to 0.1875
Outputs:
- grad_queries: bfloat16 [16, 32, 256, 1152], P('clip', 'frame')
- grad_keys: bfloat16 [16, 32, 256, 1152], P('clip', 'frame')
- grad_values: bfloat16 [16, 32, 256, 1152], P('clip', 'frame')
- grad_weight: float32 [1152, 1152], P('frame')
All inputs are finite; a program needn't handle non-finite values.
Results may differ from a plain program's by a relative error of at most 0.0058.
Values may be sent and summed in bfloat16 or wider, within the bound.
No kernel may reach another device: no remote copies, remote signals or barrier semaphores. Data moves between devices by JAX's collectives and lax.ppermute only.
A program may use at most 64 MiB of HBM per device.

v0:
```python
import jax
import jax.numpy as jnp
from jax import lax
from jax.sharding import PartitionSpec as P

HEADS = 16


def on_device(queries, keys, values, grad_out, w_out):
    spread = (
        lax.all_to_all(queries, "frame", split_axis=2, concat_axis=1, tiled=True),
        lax.all_to_all(keys, "frame", split_axis=2, concat_axis=1, tiled=True),
        lax.all_to_all(values, "frame", split_axis=2, concat_axis=1, tiled=True),
        lax.all_to_all(grad_out, "frame", split_axis=2, concat_axis=1, tiled=True),
    )
    q_local, k_local, v_local, dy_local = spread
    weight = lax.all_gather(w_out, "frame", axis=0, tiled=True)
    clips, frames, local, width = q_local.shape
    head_dim = width // HEADS
    scale = 1.0 / head_dim**0.5
    shape = (clips, frames, local, HEADS, head_dim)
    qh = q_local.reshape(shape)
    kh = k_local.reshape(shape)
    vh = v_local.reshape(shape)
    scores = jnp.einsum("cfshd,cgshd->cshfg", qh, kh, preferred_element_type=jnp.float32) * scale
    prob = jax.nn.softmax(scores, axis=-1)
    prob_b = prob.astype(jnp.bfloat16)
    attn = jnp.einsum("cshfg,cgshd->cfshd", prob_b, vh, preferred_element_type=jnp.float32).astype(
        jnp.bfloat16
    )
    attn_rows = attn.reshape(-1, width)
    dy_rows = dy_local.reshape(-1, width)
    grad_attn = jnp.einsum("te,de->td", dy_rows, weight, preferred_element_type=jnp.float32).astype(
        jnp.bfloat16
    )
    ga = grad_attn.reshape(shape)
    grad_v = jnp.einsum(
        "cshfg,cfshd->cgshd", prob_b, ga, preferred_element_type=jnp.float32
    ).astype(jnp.bfloat16)
    grad_v = grad_v.reshape(clips, frames, local, width)
    grad_prob = jnp.einsum("cfshd,cgshd->cshfg", ga, vh, preferred_element_type=jnp.float32)
    grad_scores = prob * (grad_prob - jnp.sum(prob * grad_prob, axis=-1, keepdims=True))
    gs_b = grad_scores.astype(jnp.bfloat16)
    grad_q = (
        jnp.einsum("cshfg,cgshd->cfshd", gs_b, kh, preferred_element_type=jnp.float32) * scale
    ).astype(jnp.bfloat16)
    grad_k = (
        jnp.einsum("cshfg,cfshd->cgshd", gs_b, qh, preferred_element_type=jnp.float32) * scale
    ).astype(jnp.bfloat16)
    grad_q = grad_q.reshape(clips, frames, local, width)
    grad_k = grad_k.reshape(clips, frames, local, width)
    grad_queries, grad_keys, grad_values = (
        lax.all_to_all(grad_q, "frame", split_axis=1, concat_axis=2, tiled=True),
        lax.all_to_all(grad_k, "frame", split_axis=1, concat_axis=2, tiled=True),
        lax.all_to_all(grad_v, "frame", split_axis=1, concat_axis=2, tiled=True),
    )
    members = lax.axis_size("frame")
    partial_value = lax.dot_general(
        attn_rows, dy_rows, (((0,), (0,)), ((), ())), preferred_element_type=jnp.float32
    )
    partial_value = partial_value.reshape(members, width // members, width)
    received = lax.all_to_all(partial_value, "frame", split_axis=0, concat_axis=0, tiled=True)
    owned = jnp.sum(received, axis=0)
    grad_weight = lax.psum(owned, "clip")
    return (grad_queries, grad_keys, grad_values, grad_weight)


def solution(mesh):
    in_specs = (
        P("clip", "frame", None, None),
        P("clip", "frame", None, None),
        P("clip", "frame", None, None),
        P("clip", "frame", None, None),
        P("frame", None),
    )
    out_specs = (
        P("clip", "frame", None, None),
        P("clip", "frame", None, None),
        P("clip", "frame", None, None),
        P("frame", None),
    )
    return jax.shard_map(
        on_device, mesh=mesh, in_specs=in_specs, out_specs=out_specs, check_vma=False
    )
```

profile of v0, /device:TPU:8, one launch (start us, length us, event | category | flops | bytes accessed | tf_op | source)
XLA Modules:
  0.0 537.0 jit_solution(14904103583746394235)
XLA Ops:
  11.2 4.2 reduce.13
  16.5 9.5 %all-to-all-start = ((bf16[32,2,4608]{2,1,0:T(2,128)(2,1)}), bf16[32,2,4608]{2,1,0:T(2,128)(2,1)S(1)}, u32[]{:S(2)}, u32[]{:S(2)}) async-start(bf16[32,2,4608]{2,1,0:T(2,128)(2,1)} %reshape.146), calls=%async_computation | async-start | bytes 1179648 | tf_op jit(solution)/shard_map/all_to_all | solution.py:11
  27.0 4.3 reduce.12
  32.3 15.4 %all-to-all-done = bf16[32,2,4608]{2,1,0:T(2,128)(2,1)S(1)} async-done(((bf16[32,2,4608]{2,1,0:T(2,128)(2,1)}), bf16[32,2,4608]{2,1,0:T(2,128)(2,1)S(1)}, u32[]{:S(2)}, u32[]{:S(2)}) %all-to-all-start) | async-done | bytes 589856 | tf_op jit(solution)/shard_map/all_to_all | solution.py:11
  47.6 5.3 all-to-all-start.1
  53.9 4.3 reduce.14
  59.2 15.8 %all-to-all-done.1 = bf16[32,2,4608]{2,1,0:T(2,128)(2,1)S(1)} async-done(((bf16[32,2,4608]{2,1,0:T(2,128)(2,1)}), bf16[32,2,4608]{2,1,0:T(2,128)(2,1)S(1)}, u32[]{:S(2)}, u32[]{:S(2)}) %all-to-all-start.1) | async-done | bytes 589856 | tf_op jit(solution)/shard_map/all_to_all | solution.py:12
  75.0 4.8 all-to-all-start.3
  80.7 4.2 reduce.15
  85.9 12.9 %all-to-all-done.3 = bf16[32,2,4608]{2,1,0:T(2,128)(2,1)S(1)} async-done(((bf16[32,2,4608]{2,1,0:T(2,128)(2,1)}), bf16[32,2,4608]{2,1,0:T(2,128)(2,1)S(1)}, u32[]{:S(2)}, u32[]{:S(2)}) %all-to-all-start.3) | async-done | bytes 589856 | tf_op jit(solution)/shard_map/all_to_all | solution.py:13
  98.8 5.4 all-to-all-start.2
  113.8 4.2 bitcast_reduce_fusion.1
  124.9 4.2 bitcast_reduce_fusion.2
  139.9 5.1 reshape.134
  157.7 8.4 %all-to-all-start.6 = ((bf16[1,32,8,1152]{3,2,0,1:T(8,128)(2,1)}), bf16[1,32,8,1152]{3,2,0,1:T(8,128)(2,1)}, u32[]{:S(2)}, u32[]{:S(2)}) async-start(bf16[1,32,8,1152]{3,2,0,1:T(8,128)(2,1)} %bitcast.74), calls=%async_computation.6 | async-start | bytes 1179648 | tf_op jit(solution)/shard_map/all_to_all | solution.py:55
  174.3 10.1 %all-to-all-done.6 = bf16[1,32,8,1152]{3,2,0,1:T(8,128)(2,1)} async-done(((bf16[1,32,8,1152]{3,2,0,1:T(8,128)(2,1)}), bf16[1,32,8,1152]{3,2,0,1:T(8,128)(2,1)}, u32[]{:S(2)}, u32[]{:S(2)}) %all-to-all-start.6) | async-done | bytes 589856 | tf_op jit(solution)/shard_map/all_to_all | solution.py:55
  184.4 6.1 %all-to-all-start.5 = ((bf16[1,32,8,1152]{3,2,0,1:T(8,128)(2,1)}), bf16[1,32,8,1152]{3,2,0,1:T(8,128)(2,1)}, u32[]{:S(2)}, u32[]{:S(2)}) async-start(bf16[1,32,8,1152]{3,2,0,1:T(8,128)(2,1)} %bitcast.73), calls=%async_computation.5 | async-start | bytes 1179648 | tf_op jit(solution)/shard_map/all_to_all | solution.py:54
  199.2 4.8 fusion.17
  204.0 4.7 all-to-all-done.5
  208.7 6.0 %all-to-all-start.7 = ((f32[32,36,1152]{2,1,0:T(8,128)}), f32[32,36,1152]{2,1,0:T(8,128)}, u32[]{:S(2)}, u32[]{:S(2)}) async-start(f32[32,36,1152]{2,1,0:T(8,128)} %fusion.17), calls=%async_computation.7 | async-start | bytes 11796480 | tf_op jit(solution)/shard_map/all_to_all | solution.py:62
  218.1 128.7 %all-to-all-done.7 = f32[32,36,1152]{2,1,0:T(8,128)} async-done(((f32[32,36,1152]{2,1,0:T(8,128)}), f32[32,36,1152]{2,1,0:T(8,128)}, u32[]{:S(2)}, u32[]{:S(2)}) %all-to-all-start.7) | async-done | bytes 5308448 | tf_op jit(solution)/shard_map/all_to_all | solution.py:62
  346.8 5.2 all-to-all-start.4
  355.7 14.6 %all-to-all-done.4 = bf16[1,32,8,1152]{3,2,0,1:T(8,128)(2,1)S(1)} async-done(((bf16[1,32,8,1152]{3,2,0,1:T(8,128)(2,1)}), bf16[1,32,8,1152]{3,2,0,1:T(8,128)(2,1)S(1)}, u32[]{:S(2)}, u32[]{:S(2)}) %all-to-all-start.4) | async-done | bytes 589856 | tf_op jit(solution)/shard_map/all_to_all | solution.py:53
  370.3 153.5 %all-reduce.2.cloned.1.call-done = f32[36,1152]{1,0:T(8,128)} async-done(((f32[36,1152]{1,0:T(8,128)}), f32[36,1152]{1,0:T(8,128)}) %all-reduce.2.cloned.1.call-update) | async-done | bytes 165904 | tf_op jit(solution)/shard_map/psum | solution.py:64
  (65 shorter events, 79.2 us)
Async XLA Ops:
  8.0 131.9 %all-gather.3.cloned.1.call-start = ((), (), s32[]{:S(2)}) async-start(), calls=%async_computation.9 | async-start | bytes 3041280 | tf_op jit(solution)/shard_map/all_gather | solution.py:17
  10.7 15.3 %copy-start.5 = (bf16[1,1,256,1152]{3,2,1,0:T(8,128)(2,1)S(1)}, bf16[1,1,256,1152]{3,2,1,0:T(8,128)(2,1)}, u32[]{:S(2)}) copy-start(bf16[1,1,256,1152]{3,2,1,0:T(8,128)(2,1)} %param.6) | copy-start | bytes 1769476
  16.5 31.1 %all-to-all-start = ((bf16[32,2,4608]{2,1,0:T(2,128)(2,1)}), bf16[32,2,4608]{2,1,0:T(2,128)(2,1)S(1)}, u32[]{:S(2)}, u32[]{:S(2)}) async-start(bf16[32,2,4608]{2,1,0:T(2,128)(2,1)} %reshape.146), calls=%async_computation | async-start | bytes 1179648 | tf_op jit(solution)/shard_map/all_to_all | solution.py:11
  26.9 26.0 %copy-start.6 = (bf16[1,1,256,1152]{3,2,1,0:T(8,128)(2,1)S(1)}, bf16[1,1,256,1152]{3,2,1,0:T(8,128)(2,1)}, u32[]{:S(2)}) copy-start(bf16[1,1,256,1152]{3,2,1,0:T(8,128)(2,1)} %param.7) | copy-start | bytes 1769476
  47.6 27.3 %all-to-all-start.1 = ((bf16[32,2,4608]{2,1,0:T(2,128)(2,1)}), bf16[32,2,4608]{2,1,0:T(2,128)(2,1)S(1)}, u32[]{:S(2)}, u32[]{:S(2)}) async-start(bf16[32,2,4608]{2,1,0:T(2,128)(2,1)} %reshape.144), calls=%async_computation.1 | async-start | bytes 1179648 | tf_op jit(solution)/shard_map/all_to_all | solution.py:12
  53.9 25.9 %copy-start.7 = (bf16[1,1,256,1152]{3,2,1,0:T(8,128)(2,1)S(1)}, bf16[1,1,256,1152]{3,2,1,0:T(8,128)(2,1)}, u32[]{:S(2)}) copy-start(bf16[1,1,256,1152]{3,2,1,0:T(8,128)(2,1)} %param.8) | copy-start | bytes 1769476
  75.0 9.9 %copy-start.1 = (bf16[32,2,4608]{2,1,0:T(2,128)(2,1)}, bf16[32,2,4608]{2,1,0:T(2,128)(2,1)S(1)}, u32[]{:S(2)}) copy-start(bf16[32,2,4608]{2,1,0:T(2,128)(2,1)S(1)} %all-to-all-done.1) | copy-start | bytes 1769476
  75.0 23.8 %all-to-all-start.3 = ((bf16[32,2,4608]{2,1,0:T(2,128)(2,1)}), bf16[32,2,4608]{2,1,0:T(2,128)(2,1)S(1)}, u32[]{:S(2)}, u32[]{:S(2)}) async-start(bf16[32,2,4608]{2,1,0:T(2,128)(2,1)} %reshape.140), calls=%async_computation.3 | async-start | bytes 1179648 | tf_op jit(solution)/shard_map/all_to_all | solution.py:13
  98.8 5.4 %copy-start.2 = (bf16[32,2,4608]{2,1,0:T(2,128)(2,1)}, bf16[32,2,4608]{2,1,0:T(2,128)(2,1)S(1)}, u32[]{:S(2)}) copy-start(bf16[32,2,4608]{2,1,0:T(2,128)(2,1)S(1)} %all-to-all-done.3) | copy-start | bytes 1769476
  98.8 34.0 %all-to-all-start.2 = ((bf16[32,2,4608]{2,1,0:T(2,128)(2,1)}), bf16[32,2,4608]{2,1,0:T(2,128)(2,1)}, u32[]{:S(2)}, u32[]{:S(2)}) async-start(bf16[32,2,4608]{2,1,0:T(2,128)(2,1)} %reshape.142), calls=%async_computation.2 | async-start | bytes 1179648 | tf_op jit(solution)/shard_map/all_to_all | solution.py:14
  136.6 8.4 %copy-start = (bf16[256,1,1,1152]{3,2,1,0:T(2,128)(2,1)}, bf16[256,1,1,1152]{3,2,1,0:T(2,128)(2,1)S(1)}, u32[]{:S(2)}) copy-start(bf16[256,1,1,1152]{3,2,1,0:T(2,128)(2,1)S(1)} %reshape.143) | copy-start | bytes 1769476
  151.8 1.0 copy-start.4
  157.7 26.7 %all-to-all-start.6 = ((bf16[1,32,8,1152]{3,2,0,1:T(8,128)(2,1)}), bf16[1,32,8,1152]{3,2,0,1:T(8,128)(2,1)}, u32[]{:S(2)}, u32[]{:S(2)}) async-start(bf16[1,32,8,1152]{3,2,0,1:T(8,128)(2,1)} %bitcast.74), calls=%async_computation.6 | async-start | bytes 1179648 | tf_op jit(solution)/shard_map/all_to_all | solution.py:55
  166.1 4.1 copy-start.3
  184.4 24.3 %all-to-all-start.5 = ((bf16[1,32,8,1152]{3,2,0,1:T(8,128)(2,1)}), bf16[1,32,8,1152]{3,2,0,1:T(8,128)(2,1)}, u32[]{:S(2)}, u32[]{:S(2)}) async-start(bf16[1,32,8,1152]{3,2,0,1:T(8,128)(2,1)} %bitcast.73), calls=%async_computation.5 | async-start | bytes 1179648 | tf_op jit(solution)/shard_map/all_to_all | solution.py:54
  208.7 138.1 %all-to-all-start.7 = ((f32[32,36,1152]{2,1,0:T(8,128)}), f32[32,36,1152]{2,1,0:T(8,128)}, u32[]{:S(2)}, u32[]{:S(2)}) async-start(f32[32,36,1152]{2,1,0:T(8,128)} %fusion.17), calls=%async_computation.7 | async-start | bytes 11796480 | tf_op jit(solution)/shard_map/all_to_all | solution.py:62
  346.8 23.5 %all-to-all-start.4 = ((bf16[1,32,8,1152]{3,2,0,1:T(8,128)(2,1)}), bf16[1,32,8,1152]{3,2,0,1:T(8,128)(2,1)S(1)}, u32[]{:S(2)}, u32[]{:S(2)}) async-start(bf16[1,32,8,1152]{3,2,0,1:T(8,128)(2,1)} %bitcast.4), calls=%async_computation.4 | async-start | bytes 1179648 | tf_op jit(solution)/shard_map/all_to_all | solution.py:53
  352.0 171.8 %all-reduce.2.cloned.1.call-start = ((), (), s32[]{:S(2)}) async-start(), calls=%async_computation.8 | async-start | bytes 368640 | tf_op jit(solution)/shard_map/psum | solution.py:64
  523.8 4.7 copy-start.8
Sparse Core Ops, SparseCore 0:
  11.0 80.8 all-gather.2
Sparse Core Ops, SparseCore 1:
  355.9 167.8 all-reduce.1
where the time goes:
time: 546 us; the launch traced here: 537 us
  waiting for transfers between devices  356 us (65%)
  local copies, waits for them, and re-layouts  69.8 us (13%)
  starting transfers between devices  50.6 us (9%)
  matrix products  22.7 us (4%)
  other arithmetic  21.3 us (4%)
  between operations  16.3 us (3%)
    psum x1, waiting for transfers between devices, on_device(): grad_weight = lax.psum(owned, 'clip')  153 us
    all_to_all x1, waiting for transfers between devices, on_device(): lax.all_to_all(partial_value, 'frame', split_axis=0, concat_axis=0, tiled...  129 us
    unnamed x36, local copies, waits for them, and re-layouts  32.9 us
    unnamed x4, other arithmetic  17 us
    all_to_all x1, waiting for transfers between devices, on_device(): lax.all_to_all(keys, 'frame', split_axis=2, concat_axis=1, tiled=True)  15.8 us
    all_to_all x1, waiting for transfers between devices, on_device(): lax.all_to_all(queries, 'frame', split_axis=2, concat_axis=1, tiled=True)  15.4 us
    all_to_all x1, waiting for transfers between devices, on_device(): lax.all_to_all(grad_q, 'frame', split_axis=1, concat_axis=2, tiled=True)  14.6 us
    all_to_all x1, waiting for transfers between devices, on_device(): lax.all_to_all(values, 'frame', split_axis=2, concat_axis=1, tiled=True)  12.9 us
  transfers between devices with their start and end apart: 10, of which 8 were waited for; matrix products, arithmetic and copies ran while one was open for 17% of the time, Pallas kernels for 0%

commit v1 on v0

v1 whole, which is shorter than its diff:
```python
import jax
import jax.numpy as jnp
from jax import lax
from jax.experimental import pallas as pl
from jax.experimental.pallas import tpu as pltpu
from jax.sharding import PartitionSpec as P

HEADS = 16
HEAD_DIM = 72
WIDTH = 1152
FRAMES = 32
SLOTS = 8
TOKENS = FRAMES * SLOTS
ROWS = 36
QUARTER = ROWS // 4
HALF = 640
SCALE = 1.0 / HEAD_DIM**0.5
LANES = 128
PIECES = ((0, 1, 2), (3, 4), (5, 6), (7, 8))
VMEM = 56 * 1024 * 1024
NN = (((1,), (0,)), ((), ()))
NT = (((1,), (1,)), ((), ()))
TN = (((0,), (0,)), ((), ()))


def mm(a, b, dims):
    return lax.dot_general(a, b, dims, preferred_element_type=jnp.float32)


def window(head):
    first, last = head * HEAD_DIM, (head + 1) * HEAD_DIM - 1
    return first // LANES, last // LANES + 1


def head_mask(head):
    lo, hi = window(head)
    lane = lax.broadcasted_iota(jnp.int32, (1, (hi - lo) * LANES), 1) + lo * LANES
    own = (lane >= head * HEAD_DIM) & (lane < (head + 1) * HEAD_DIM)
    return jnp.where(own, 1.0, 0.0).astype(jnp.bfloat16)


def same_position():
    row = lax.broadcasted_iota(jnp.int32, (TOKENS, TOKENS), 0)
    col = lax.broadcasted_iota(jnp.int32, (TOKENS, TOKENS), 1)
    return jnp.where((row & (SLOTS - 1)) == (col & (SLOTS - 1)), 0.0, -1e30)


def load_tokens(got_ref, which):
    x = got_ref[:, which].astype(jnp.float32).reshape(TOKENS, WIDTH)
    return x.astype(jnp.bfloat16)


class Tiles:
    def __init__(self, store):
        self.open, self.store = {}, store

    def add(self, head, value):
        lo, hi = window(head)
        for tile in range(lo, hi):
            part = value[:, (tile - lo) * LANES : (tile - lo + 1) * LANES]
            self.open[tile] = self.open[tile] + part if tile in self.open else part
        keep = window(head + 1)[0] if head + 1 < HEADS else WIDTH // LANES
        for tile in sorted(self.open):
            if tile < keep:
                self.store(tile, self.open.pop(tile))


def pack_kernel(q_ref, k_ref, v_ref, dy_ref, out_ref, sems):
    copies = [
        pltpu.make_async_copy(ref, out_ref.at[:, i], sems.at[i])
        for i, ref in enumerate((q_ref, k_ref, v_ref, dy_ref))
    ]
    for copy in copies:
        copy.start()
    for copy in copies:
        copy.wait()


def pack(*arrays):
    return pl.pallas_call(
        pack_kernel,
        out_shape=jax.ShapeDtypeStruct((FRAMES, 4, SLOTS, WIDTH), jnp.bfloat16),
        in_specs=[pl.BlockSpec(memory_space=pl.ANY)] * 4,
        out_specs=pl.BlockSpec(memory_space=pltpu.VMEM),
        scratch_shapes=[pltpu.SemaphoreType.DMA((4,))],
        compiler_params=pltpu.CompilerParams(vmem_limit_bytes=VMEM),
        name="pack",
    )(*[a.reshape(FRAMES, SLOTS, WIDTH) for a in arrays])


def forward_kernel(got_ref, order_ref, dy_ref, attn_ref, stats_ref, q_ref, k_ref, v_ref, plain_ref):
    q_ref[...] = load_tokens(got_ref, 0)
    k_ref[...] = load_tokens(got_ref, 1)
    v_ref[...] = load_tokens(got_ref, 2)
    dy_ref[...] = load_tokens(got_ref, 3)
    bias = same_position()

    def store(tile, value):
        plain_ref[:, tile * LANES : (tile + 1) * LANES] = value.astype(jnp.bfloat16)

    attn = Tiles(store)
    lane = lax.broadcasted_iota(jnp.int32, (TOKENS, LANES), 1)
    stats = jnp.zeros((TOKENS, LANES), jnp.float32)
    for head in range(HEADS):
        lo, hi = window(head)
        cols = slice(lo * LANES, hi * LANES)
        mask = head_mask(head)
        scores = mm(q_ref[:, cols], k_ref[:, cols] * mask, NT) * SCALE + bias
        top = jnp.max(scores, axis=1, keepdims=True)
        weight = jnp.exp(scores - top)
        inverse = 1.0 / jnp.sum(weight, axis=1, keepdims=True)
        prob = (weight * inverse).astype(jnp.bfloat16)
        attn.add(head, mm(prob, v_ref[:, cols] * mask, NN))
        stats = jnp.where(lane == head, top, stats)
        stats = jnp.where(lane == HEADS + head, inverse, stats)
    stats_ref[...] = stats.T
    for core in range(2):
        cols = slice(core * HALF, (core + 1) * HALF)
        attn_ref[core] = mm(plain_ref[...], order_ref[:, cols], NN).astype(jnp.bfloat16)


def selection():
    row = lax.broadcasted_iota(jnp.int32, (WIDTH, 2 * HALF), 0)
    col = lax.broadcasted_iota(jnp.int32, (WIDTH, 2 * HALF), 1)
    block, within = row // ROWS, row % ROWS
    place = (block % 2) * HALF + (within // QUARTER) * 144 + (block // 2) * QUARTER + within % QUARTER
    return (place == col).astype(jnp.bfloat16)


def forward(got, order):
    tokens = pltpu.VMEM((TOKENS, WIDTH), jnp.bfloat16)
    return pl.pallas_call(
        forward_kernel,
        out_shape=(
            jax.ShapeDtypeStruct((TOKENS, WIDTH), jnp.bfloat16),
            jax.ShapeDtypeStruct((2, TOKENS, HALF), jnp.bfloat16),
            jax.ShapeDtypeStruct((LANES, TOKENS), jnp.float32),
        ),
        in_specs=[pl.BlockSpec(memory_space=pltpu.VMEM)] * 2,
        out_specs=[pl.BlockSpec(memory_space=pltpu.VMEM)] * 3,
        scratch_shapes=[tokens] * 4,
        compiler_params=pltpu.CompilerParams(vmem_limit_bytes=VMEM),
        name="attention",
    )(got, order)


def backward_kernel(got_ref, dy_ref, stats_ref, w_ref, out_ref, q_ref, k_ref, v_ref, ga_ref, rows_ref):
    q_ref[...] = load_tokens(got_ref, 0)
    k_ref[...] = load_tokens(got_ref, 1)
    v_ref[...] = load_tokens(got_ref, 2)
    for block in range(FRAMES):
        rows_ref[block * ROWS : (block + 1) * ROWS, :] = w_ref[block]
    for tile in range(WIDTH // LANES):
        cols = slice(tile * LANES, (tile + 1) * LANES)
        ga_ref[:, cols] = mm(dy_ref[...], rows_ref[cols, :], NT).astype(jnp.bfloat16)
    bias = same_position()

    def storer(which, scale):
        def store(tile, value):
            if scale is not None:
                value = value * scale
            out_ref[:, which, :, tile * LANES : (tile + 1) * LANES] = value.reshape(
                FRAMES, SLOTS, LANES
            ).astype(jnp.bfloat16)

        return store

    grad_q, grad_k = Tiles(storer(0, SCALE)), Tiles(storer(1, SCALE))
    grad_v = Tiles(storer(2, None))
    for head in range(HEADS):
        lo, hi = window(head)
        cols = slice(lo * LANES, hi * LANES)
        mask = head_mask(head)
        q, k, v, ga = q_ref[:, cols], k_ref[:, cols], v_ref[:, cols], ga_ref[:, cols]
        k_own, ga_own = k * mask, ga * mask
        scores = mm(k_own, q, NT) * SCALE + bias
        top = stats_ref[head : head + 1, :]
        inverse = stats_ref[HEADS + head : HEADS + head + 1, :]
        prob = jnp.exp(scores - top) * inverse
        grad_v.add(head, mm(prob.astype(jnp.bfloat16), ga_own, NN))
        product = prob * mm(v, ga_own, NT)
        total = jnp.sum(product, axis=0, keepdims=True)
        grad_scores = (product - prob * total).astype(jnp.bfloat16)
        grad_k.add(head, mm(grad_scores, q * mask, NN))
        grad_q.add(head, mm(grad_scores, k_own, TN))


def backward(got, dy, stats, weight):
    tokens = pltpu.VMEM((TOKENS, WIDTH), jnp.bfloat16)
    return pl.pallas_call(
        backward_kernel,
        out_shape=jax.ShapeDtypeStruct((FRAMES, 3, SLOTS, WIDTH), jnp.bfloat16),
        in_specs=[pl.BlockSpec(memory_space=pltpu.VMEM)] * 4,
        out_specs=pl.BlockSpec(memory_space=pltpu.VMEM),
        scratch_shapes=[tokens] * 4 + [pltpu.VMEM((WIDTH, WIDTH), jnp.bfloat16)],
        compiler_params=pltpu.CompilerParams(vmem_limit_bytes=VMEM),
        name="attention_gradients",
    )(got, dy, stats, weight)


def weight_kernel(place_ref, attn_ref, attn_in_ref, dy_ref, dy_in_ref, out_ref):
    own = attn_ref[place_ref[0]]
    for tile in range(WIDTH // LANES):
        cols = slice(tile * LANES, (tile + 1) * LANES)
        total = mm(own, dy_ref[:, cols], TN) + mm(attn_in_ref[...], dy_in_ref[:, cols], TN)
        for x in range(4):
            slot = (x - place_ref[1]) & 3
            out_ref[slot, :, cols] = total[x * 144 : (x + 1) * 144].astype(jnp.bfloat16)


def weight_term(place, attn, attn_in, dy, dy_in):
    return pl.pallas_call(
        weight_kernel,
        out_shape=jax.ShapeDtypeStruct((4, 144, WIDTH), jnp.bfloat16),
        in_specs=[pl.BlockSpec(memory_space=pltpu.SMEM)]
        + [pl.BlockSpec(memory_space=pltpu.VMEM)] * 4,
        out_specs=pl.BlockSpec(memory_space=pltpu.VMEM),
        compiler_params=pltpu.CompilerParams(vmem_limit_bytes=VMEM),
        name="weight_term",
    )(place, attn, attn_in, dy, dy_in)


def add_x_kernel(place_ref, a_ref, b_ref, c_ref, d_ref, out_ref):
    for piece, tiles in enumerate(PIECES):
        slot = (piece - place_ref[2]) & 3
        for i in range(3):
            if i < len(tiles):
                cols = slice(tiles[i] * LANES, (tiles[i] + 1) * LANES)
                parts = [r[:, cols].astype(jnp.float32) for r in (a_ref, b_ref, c_ref, d_ref)]
                total = (parts[0] + parts[1]) + (parts[2] + parts[3])
            else:
                total = jnp.zeros((144, LANES), jnp.float32)
            out_ref[slot, :, i * LANES : (i + 1) * LANES] = total.astype(jnp.bfloat16)


def add_x(place, parts):
    return pl.pallas_call(
        add_x_kernel,
        out_shape=jax.ShapeDtypeStruct((4, 144, 3 * LANES), jnp.bfloat16),
        in_specs=[pl.BlockSpec(memory_space=pltpu.SMEM)]
        + [pl.BlockSpec(memory_space=pltpu.VMEM)] * 4,
        out_specs=pl.BlockSpec(memory_space=pltpu.VMEM),
        name="add_x",
    )(place, *parts)


def add_z_kernel(a_ref, b_ref, c_ref, d_ref, out_ref):
    for i in range(3):
        cols = slice(i * LANES, (i + 1) * LANES)
        parts = [r[:, cols].astype(jnp.float32) for r in (a_ref, b_ref, c_ref, d_ref)]
        total = (parts[0] + parts[1]) + (parts[2] + parts[3])
        for block in range(16):
            out_ref[block, i * QUARTER : (i + 1) * QUARTER, :] = total[
                block * QUARTER : (block + 1) * QUARTER
            ]
    out_ref[:, 3 * QUARTER :, :] = jnp.zeros((16, 5, LANES), jnp.float32)


def add_z(parts):
    return pl.pallas_call(
        add_z_kernel,
        out_shape=jax.ShapeDtypeStruct((16, 32, LANES), jnp.float32),
        in_specs=[pl.BlockSpec(memory_space=pltpu.VMEM)] * 4,
        out_specs=pl.BlockSpec(memory_space=pltpu.VMEM),
        name="add_z",
    )(*parts)


def add_frames_kernel(got_ref, out_ref):
    total = jnp.sum(got_ref[...], axis=0)
    for i in range(16):
        out_ref[i] = total


def add_frames(got):
    return pl.pallas_call(
        add_frames_kernel,
        out_shape=jax.ShapeDtypeStruct((16, 32, LANES), jnp.float32),
        in_specs=[pl.BlockSpec(memory_space=pltpu.VMEM)],
        out_specs=pl.BlockSpec(memory_space=pltpu.VMEM),
        name="add_frames",
    )(got)


def assemble_kernel(got_ref, out_ref):
    for piece, tiles in enumerate(PIECES):
        for x in range(4):
            for i, tile in enumerate(tiles):
                out_ref[x * QUARTER : (x + 1) * QUARTER, tile * LANES : (tile + 1) * LANES] = got_ref[
                    piece * 4 + x, i * QUARTER : (i + 1) * QUARTER, :
                ]


def assemble(got):
    return pl.pallas_call(
        assemble_kernel,
        out_shape=jax.ShapeDtypeStruct((ROWS, WIDTH), jnp.float32),
        in_specs=[pl.BlockSpec(memory_space=pltpu.VMEM)],
        out_specs=pl.BlockSpec(memory_space=pltpu.VMEM),
        name="assemble",
    )(got)


def at(y, z, core):
    return y * 4 + z * 2 + core


SWAP_CORE = [(i, i ^ 1) for i in range(FRAMES)]
SAME_CORE = [[at(y, z, c) for y in range(8) for z in range(2)] for c in range(2)]


def all_to_all(x, axis, groups=None):
    return lax.all_to_all(
        x, axis, split_axis=0, concat_axis=0, tiled=True, axis_index_groups=groups
    )


def along_x(x, step):
    return lax.ppermute(
        x, "clip", [(z * 4 + i, z * 4 + (i + step) % 4) for z in range(4) for i in range(4)]
    )


def along_z(x, step):
    return lax.ppermute(
        x, "clip", [(z * 4 + i, (z + step) % 4 * 4 + i) for z in range(4) for i in range(4)]
    )


def on_device(queries, keys, values, grad_out, w_out):
    weight = lax.all_gather(w_out, "frame", axis=0)
    got = all_to_all(pack(queries, keys, values, grad_out), "frame")
    dy, attn, stats = forward(got, selection())

    core = lax.axis_index("frame") & 1
    clip = lax.axis_index("clip")
    place = jnp.stack([core, clip & 3, clip >> 2])
    attn_in = lax.ppermute(lax.dynamic_index_in_dim(attn, 1 - core, 0, False), "frame", SWAP_CORE)
    dy_in = lax.ppermute(dy, "frame", SWAP_CORE)
    term = weight_term(place, attn, attn_in, dy, dy_in)
    term = add_x(place, [term[0]] + [along_x(term[i], i) for i in (1, 2, 3)])
    term = add_z([term[0]] + [along_z(term[i], i) for i in (1, 2, 3)])

    out = all_to_all(backward(got, dy, stats, weight), "frame")

    out, term = lax.optimization_barrier((out, term))
    term = add_frames(all_to_all(term, "frame", SAME_CORE))
    grad_weight = assemble(all_to_all(term, "clip"))
    shape = (1, 1, TOKENS, WIDTH)
    return (
        out[:, 0].reshape(shape),
        out[:, 1].reshape(shape),
        out[:, 2].reshape(shape),
        grad_weight,
    )


def solution(mesh):
    spread = P("clip", "frame", None, None)
    return jax.shard_map(
        on_device,
        mesh=mesh,
        in_specs=(spread, spread, spread, spread, P("frame", None)),
        out_specs=(spread, spread, spread, P("frame", None)),
        check_vma=False,
    )
```

time: 546 us -> 240 us (0.44); the launches traced: 537 us -> 239 us
  waiting for transfers between devices: 356 us -> 99.5 us
  local copies, waits for them, and re-layouts: 69.8 us -> 9.4 us
  Pallas kernels: 0 us -> 33.3 us
  matrix products: 22.7 us -> 0 us
  blocking collectives: 0 us -> 17.7 us
  other arithmetic: 21.3 us -> 6.64 us
  starting transfers between devices: 50.6 us -> 58.4 us
    psum x1 -> x0, waiting for transfers between devices: 153 us -> none  [on_device(): grad_weight = lax.psum(owned, 'clip')]
    all_to_all x8 -> x3, waiting for transfers between devices: 202 us -> 68.2 us  [all_to_all(): lax.all_to_all(x, axis, split_axis=0, concat_axis=0, tiled=True, axis_ind...]
    pallas_call x0 -> x8, Pallas kernels: none -> 33.3 us  [the longest x1 11.1 us: backward(): pl.pallas_call(backward_kernel, out_shape=jax.ShapeDtypeStruct((FRAMES, 3...]
    ppermute x0 -> x8, starting transfers between devices: none -> 32.4 us  [the longest x3 16.6 us: along_z(): lax.ppermute(x, 'clip', [(z * 4 + i, (z + step) % 4 * 4 + i) for z in ran...]
    unnamed x36 -> x22, local copies, waits for them, and re-layouts: 32.9 us -> 4.27 us
    all_to_all x8 -> x3, starting transfers between devices: 50.6 us -> 25.9 us  [all_to_all(): lax.all_to_all(x, axis, split_axis=0, concat_axis=0, tiled=True, axis_ind...]
    dot_general x7 -> x0, matrix products: 19.5 us -> none  [the longest x1 4.83 us: on_device(): lax.dot_general(attn_rows, dy_rows, (((0,), (0,)), ((), ())), preferred_e...]
    all_to_all x0 -> x1, blocking collectives: none -> 17.7 us  [all_to_all(): lax.all_to_all(x, axis, split_axis=0, concat_axis=0, tiled=True, axis_ind...]
  transfers between devices with their start and end apart: 10 -> 12, of which waited for: 8 -> 9; matrix products, arithmetic and copies ran while one was open for 17% -> 5% of each run, Pallas kernels for 0% -> 7%
where the time goes in v1:
time: 240 us; the launch traced here: 239 us
  waiting for transfers between devices  99.5 us (41%)
  starting transfers between devices  58.4 us (24%)
  Pallas kernels  33.3 us (14%)
  blocking collectives  17.7 us (7%)
  between operations  14.2 us (6%)
  local copies, waits for them, and re-layouts  9.4 us (4%)
  other arithmetic  6.64 us (3%)
    all_to_all x3, waiting for transfers between devices, all_to_all(): lax.all_to_all(x, axis, split_axis=0, concat_axis=0, tiled=True, axis_ind...  68.2 us
    all_to_all x3, starting transfers between devices, all_to_all(): lax.all_to_all(x, axis, split_axis=0, concat_axis=0, tiled=True, axis_ind...  25.9 us
    all_to_all x1, blocking collectives, all_to_all(): lax.all_to_all(x, axis, split_axis=0, concat_axis=0, tiled=True, axis_ind...  17.7 us
    ppermute x3, starting transfers between devices, along_z(): lax.ppermute(x, 'clip', [(z * 4 + i, (z + step) % 4 * 4 + i) for z in ran...  16.6 us
    all_gather x1, waiting for transfers between devices, on_device(): weight = lax.all_gather(w_out, 'frame', axis=0)  13.6 us
    ppermute x3, waiting for transfers between devices, along_x(): lax.ppermute(x, 'clip', [(z * 4 + i, z * 4 + (i + step) % 4) for z in ran...  11.5 us
    ppermute x3, starting transfers between devices, along_x(): lax.ppermute(x, 'clip', [(z * 4 + i, z * 4 + (i + step) % 4) for z in ran...  11.3 us
    pallas_call x1, Pallas kernels, backward(): pl.pallas_call(backward_kernel, out_shape=jax.ShapeDtypeStruct((FRAMES, 3...  11.1 us
  transfers between devices with their start and end apart: 12, of which 9 were waited for; matrix products, arithmetic and copies ran while one was open for 5% of the time, Pallas kernels for 7%

profile of v1, /device:TPU:8, one launch (start us, length us, event | category | flops | bytes accessed | tf_op | source)
XLA Modules:
  0.0 239.2 jit_solution(10753408250448548256)
XLA Ops:
  7.2 3.1 %pack.1 = bf16[32,4,8,1152]{3,2,1,0:T(8,128)(2,1)} custom-call(bf16[32,8,1152]{2,1,0:T(8,128)(2,1)} %bitcast.32, bf16[32,8,1152]{2,1,0:T(8,128)(2,1)} %bitcast.33, bf16[32,8,1152]{2,1,0:T(8,128)(2,1)} %bitcast.34, bf16[32,8,1152]{2,1,0:T(8,128)(2,1)} %bitcast.35), custom_call_target="tpu_custom_call" | custom-call | tf_op jit(solution)/shard_map/pack/pallas_call | solution.py:80
  10.3 9.6 %all-to-all-start = ((bf16[32,4,8,1152]{3,2,1,0:T(8,128)(2,1)}), bf16[32,4,8,1152]{3,2,1,0:T(8,128)(2,1)S(1)}, u32[]{:S(2)}, u32[]{:S(2)}) async-start(bf16[32,4,8,1152]{3,2,1,0:T(8,128)(2,1)} %pack.1), calls=%async_computation | async-start | bytes 4718592 | tf_op jit(solution)/shard_map/all_to_all | solution.py:313
  20.6 6.0 %fusion.18.order_ref = bf16[1152,1280]{1,0:T(8,128)(2,1)} fusion(s32[1152]{0:T(1024)S(1)} %get-tuple-element.26, s32[1152]{0:T(1024)S(1)} %get-tuple-element.27, s32[1152]{0:T(1024)S(1)} %get-tuple-element.25, s32[1152]{0:T(1024)S(1)} %get-tuple-element.28, pred[1152]{0:T(1024)(128)(4,1)S(1)} %get-tuple-element.29, pred[1152]{0:T(1024)(128)(4,1)S(1)} %get-tuple-element.30), kind=kLoop, calls=%fused_computation.30 | loop fusion | flops 60456960 | bytes 2969856 | tf_op jit(solution)/shard_map/convert_element_type | solution.py:127
  26.6 58.3 %all-to-all-done.got_ref = bf16[32,4,8,1152]{3,2,1,0:T(8,128)(2,1)S(1)} async-done(((bf16[32,4,8,1152]{3,2,1,0:T(8,128)(2,1)}), bf16[32,4,8,1152]{3,2,1,0:T(8,128)(2,1)S(1)}, u32[]{:S(2)}, u32[]{:S(2)}) %all-to-all-start) | async-done | bytes 2359328 | tf_op jit(solution)/shard_map/all_to_all | solution.py:313
  86.3 7.4 %attention.1 = (bf16[256,1152]{1,0:T(8,128)(2,1)}, bf16[2,256,640]{2,1,0:T(8,128)(2,1)}, f32[128,256]{1,0:T(8,128)}) custom-call(bf16[32,4,8,1152]{3,2,1,0:T(8,128)(2,1)} %copy-done, bf16[1152,1280]{1,0:T(8,128)(2,1)} %fusion.18.order_ref), custom_call_target="tpu_custom_call" | custom-call | tf_op jit(solution)/shard_map/attention/pallas_call | solution.py:132
  93.7 13.6 %all-gather.4.cloned.1.call-done.w_ref = bf16[32,36,1152]{2,1,0:T(8,128)(2,1)} async-done(((bf16[1,36,1152]{2,1,0:T(8,128)(2,1)}), bf16[32,36,1152]{2,1,0:T(8,128)(2,1)}) %all-gather.4.cloned.1.call-update) | async-done | bytes 2654224 | tf_op jit(solution)/shard_map/all_gather | solution.py:331
  107.3 11.1 %attention_gradients.1 = bf16[32,3,8,1152]{3,2,1,0:T(8,128)(2,1)} custom-call(bf16[32,4,8,1152]{3,2,1,0:T(8,128)(2,1)} %copy-done, bf16[256,1152]{1,0:T(8,128)(2,1)} %get-tuple-element.9.dy_ref, f32[128,256]{1,0:T(8,128)} %get-tuple-element.10.stats_ref, bf16[32,36,1152]{2,1,0:T(8,128)(2,1)} %all-gather.4.cloned.1.call-done.w_ref), custom_call_target="tpu_custom_call" | custom-call | tf_op jit(solution)/shard_map/attention_gradients/pallas_call | solution.py:190
  118.4 6.8 %all-to-all-start.1 = ((bf16[32,3,8,1152]{3,2,1,0:T(8,128)(2,1)}), bf16[32,3,8,1152]{3,2,1,0:T(8,128)(2,1)S(1)}, u32[]{:S(2)}, u32[]{:S(2)}) async-start(bf16[32,3,8,1152]{3,2,1,0:T(8,128)(2,1)} %attention_gradients.1), calls=%async_computation.1 | async-start | bytes 3538944 | tf_op jit(solution)/shard_map/all_to_all | solution.py:313
  125.2 2.1 collective-permute-start.1
  127.4 2.5 %collective-permute-start = (bf16[256,640]{1,0:T(8,128)(2,1)S(1)}, bf16[256,640]{1,0:T(8,128)(2,1)S(1)}, u32[]{:S(2)}, u32[]{:S(2)}) collective-permute-start(bf16[256,640]{1,0:T(8,128)(2,1)S(1)} %dynamic-slice_bitcast_fusion), channel_id=1, source_target_pairs={{0,1},{1,0},{2,3},{3,2},{4,5},{5,4},{6,7},{7,6},{8,9},{9,8},{10,11... | collective-permute-start | bytes 983048 | tf_op jit(solution)/shard_map/ppermute | solution.py:338
  131.6 4.4 %weight_term.1 = bf16[4,144,1152]{2,1,0:T(8,128)(2,1)} custom-call(s32[3]{0:T(128)} %pad_add_fusion.place_ref, bf16[2,256,640]{2,1,0:T(8,128)(2,1)} %get-tuple-element.11.attn_ref, bf16[256,640]{1,0:T(8,128)(2,1)} %copy-done.7, bf16[256,1152]{1,0:T(8,128)(2,1)} %get-tuple-element.9.dy_ref, bf16[256,1152]{1,0:T(8,128)(2,1)} %collective-permute-done.1.dy_in_ref), custom_call_target="tpu_custom_call" | custom-call | tf_op jit(solution)/shard_map/weight_term/pallas_call | solution.py:212
  136.0 2.1 slice_bitcast_fusion.3
  138.1 3.9 %collective-permute-start.2 = (bf16[144,1152]{1,0:T(8,128)(2,1)S(1)}, bf16[144,1152]{1,0:T(8,128)(2,1)S(1)}, u32[]{:S(2)}, u32[]{:S(2)}) collective-permute-start(bf16[144,1152]{1,0:T(8,128)(2,1)S(1)} %get-tuple-element.19), channel_id=1, source_target_pairs={{0,32},{32,64},{64,96},{96,0},{128,160},{160,192},{192,224},{224,1... | collective-permute-start | bytes 995336 | tf_op jit(solution)/shard_map/ppermute | solution.py:319
  142.0 4.0 %collective-permute-start.3 = (bf16[144,1152]{1,0:T(8,128)(2,1)S(1)}, bf16[144,1152]{1,0:T(8,128)(2,1)S(1)}, u32[]{:S(2)}, u32[]{:S(2)}) collective-permute-start(bf16[144,1152]{1,0:T(8,128)(2,1)S(1)} %get-tuple-element.18), channel_id=1, source_target_pairs={{0,64},{32,96},{64,0},{96,32},{128,192},{160,224},{192,128},{224,1... | collective-permute-start | bytes 995336 | tf_op jit(solution)/shard_map/ppermute | solution.py:319
  146.0 3.4 %collective-permute-start.4 = (bf16[144,1152]{1,0:T(8,128)(2,1)S(1)}, bf16[144,1152]{1,0:T(8,128)(2,1)S(1)}, u32[]{:S(2)}, u32[]{:S(2)}) collective-permute-start(bf16[144,1152]{1,0:T(8,128)(2,1)S(1)} %get-tuple-element.17), channel_id=1, source_target_pairs={{0,96},{32,0},{64,32},{96,64},{128,224},{160,128},{192,160},{224,1... | collective-permute-start | bytes 995336 | tf_op jit(solution)/shard_map/ppermute | solution.py:319
  151.2 8.0 %collective-permute-done.3.c_ref = bf16[144,1152]{1,0:T(8,128)(2,1)S(1)} collective-permute-done((bf16[144,1152]{1,0:T(8,128)(2,1)S(1)}, bf16[144,1152]{1,0:T(8,128)(2,1)S(1)}, u32[]{:S(2)}, u32[]{:S(2)}) %collective-permute-start.3) | collective-permute-done | bytes 331808 | tf_op jit(solution)/shard_map/ppermute | solution.py:319
  161.6 2.2 add_x.1
  165.6 5.1 %collective-permute-start.5 = (bf16[144,384]{1,0:T(8,128)(2,1)S(1)}, bf16[144,384]{1,0:T(8,128)(2,1)S(1)}, u32[]{:S(2)}, u32[]{:S(2)}) collective-permute-start(bf16[144,384]{1,0:T(8,128)(2,1)S(1)} %get-tuple-element.23), channel_id=1, source_target_pairs={{0,128},{32,160},{64,192},{96,224},{128,256},{160,288},{192,320},{... | collective-permute-start | bytes 331784 | tf_op jit(solution)/shard_map/ppermute | solution.py:325
  170.7 6.1 %collective-permute-start.6 = (bf16[144,384]{1,0:T(8,128)(2,1)S(1)}, bf16[144,384]{1,0:T(8,128)(2,1)S(1)}, u32[]{:S(2)}, u32[]{:S(2)}) collective-permute-start(bf16[144,384]{1,0:T(8,128)(2,1)S(1)} %get-tuple-element.22), channel_id=1, source_target_pairs={{0,256},{32,288},{64,320},{96,352},{128,384},{160,416},{192,448},{... | collective-permute-start | bytes 331784 | tf_op jit(solution)/shard_map/ppermute | solution.py:325
  176.7 5.4 %collective-permute-start.7 = (bf16[144,384]{1,0:T(8,128)(2,1)S(1)}, bf16[144,384]{1,0:T(8,128)(2,1)S(1)}, u32[]{:S(2)}, u32[]{:S(2)}) collective-permute-start(bf16[144,384]{1,0:T(8,128)(2,1)S(1)} %get-tuple-element.21), channel_id=1, source_target_pairs={{0,384},{32,416},{64,448},{96,480},{128,0},{160,32},{192,64},{224,... | collective-permute-start | bytes 331784 | tf_op jit(solution)/shard_map/ppermute | solution.py:325
  183.2 4.2 %collective-permute-done.7.d_ref = bf16[144,384]{1,0:T(8,128)(2,1)S(1)} collective-permute-done((bf16[144,384]{1,0:T(8,128)(2,1)S(1)}, bf16[144,384]{1,0:T(8,128)(2,1)S(1)}, u32[]{:S(2)}, u32[]{:S(2)}) %collective-permute-start.7) | collective-permute-done | bytes 110624 | tf_op jit(solution)/shard_map/ppermute | solution.py:325
  189.8 17.7 %all_to_all.20.got_ref = f32[16,32,128]{2,1,0:T(8,128)} all-to-all(f32[16,32,128]{2,1,0:T(8,128)} %add_z.1), channel_id=1, replica_groups={{0,2,4,6,8,10,12,14,16,18,20,22,24,26,28,30},{1,3,5,7,9,11,13,15,17,19,..., dimensions={0} | all-to-all | bytes 524288 | tf_op jit(solution)/shard_map/all_to_all | solution.py:313
  209.3 9.6 %all-to-all-start.3 = ((f32[16,32,128]{2,1,0:T(8,128)}), f32[16,32,128]{2,1,0:T(8,128)S(1)}, u32[]{:S(2)}, u32[]{:S(2)}) async-start(f32[16,32,128]{2,1,0:T(8,128)} %add_frames.1), calls=%async_computation.3 | async-start | bytes 524288 | tf_op jit(solution)/shard_map/all_to_all | solution.py:313
  220.1 9.9 %all-to-all-done.3.got_ref = f32[16,32,128]{2,1,0:T(8,128)S(1)} async-done(((f32[16,32,128]{2,1,0:T(8,128)}), f32[16,32,128]{2,1,0:T(8,128)S(1)}, u32[]{:S(2)}, u32[]{:S(2)}) %all-to-all-start.3) | async-done | bytes 262176 | tf_op jit(solution)/shard_map/all_to_all | solution.py:313
  (41 shorter events, 18.7 us)
Async XLA Ops:
  10.3 74.6 %all-to-all-start = ((bf16[32,4,8,1152]{3,2,1,0:T(8,128)(2,1)}), bf16[32,4,8,1152]{3,2,1,0:T(8,128)(2,1)S(1)}, u32[]{:S(2)}, u32[]{:S(2)}) async-start(bf16[32,4,8,1152]{3,2,1,0:T(8,128)(2,1)} %pack.1), calls=%async_computation | async-start | bytes 4718592 | tf_op jit(solution)/shard_map/all_to_all | solution.py:313
  19.9 87.5 %all-gather.4.cloned.1.call-start = ((), (), s32[]{:S(2)}) async-start(), calls=%async_computation.4 | async-start | bytes 3041280 | tf_op jit(solution)/shard_map/all_gather | solution.py:331
  84.9 1.5 copy-start
  118.4 6.8 %copy-start.1 = (bf16[256,1152]{1,0:T(8,128)(2,1)S(1)}, bf16[256,1152]{1,0:T(8,128)(2,1)}, u32[]{:S(2)}) copy-start(bf16[256,1152]{1,0:T(8,128)(2,1)} %get-tuple-element.9.dy_ref) | copy-start | bytes 1769476
  118.4 8.9 %copy-start.2 = (bf16[2,256,640]{2,1,0:T(8,128)(2,1)S(1)}, bf16[2,256,640]{2,1,0:T(8,128)(2,1)}, u32[]{:S(2)}) copy-start(bf16[2,256,640]{2,1,0:T(8,128)(2,1)} %get-tuple-element.11.attn_ref) | copy-start | bytes 1966084
  118.4 71.5 %all-to-all-start.1 = ((bf16[32,3,8,1152]{3,2,1,0:T(8,128)(2,1)}), bf16[32,3,8,1152]{3,2,1,0:T(8,128)(2,1)S(1)}, u32[]{:S(2)}, u32[]{:S(2)}) async-start(bf16[32,3,8,1152]{3,2,1,0:T(8,128)(2,1)} %attention_gradients.1), calls=%async_computation.1 | async-start | bytes 3538944 | tf_op jit(solution)/shard_map/all_to_all | solution.py:313
  125.2 5.7 %collective-permute-start.1 = (bf16[256,1152]{1,0:T(8,128)(2,1)S(1)}, bf16[256,1152]{1,0:T(8,128)(2,1)}, u32[]{:S(2)}, u32[]{:S(2)}) collective-permute-start(bf16[256,1152]{1,0:T(8,128)(2,1)S(1)} %copy-done.1), channel_id=1, source_target_pairs={{0,1},{1,0},{2,3},{3,2},{4,5},{5,4},{6,7},{7,6},{8,9},{9,8},{10,11... | collective-permute-start | bytes 1769480 | tf_op jit(solution)/shard_map/ppermute | solution.py:339
  127.4 3.5 %collective-permute-start = (bf16[256,640]{1,0:T(8,128)(2,1)S(1)}, bf16[256,640]{1,0:T(8,128)(2,1)S(1)}, u32[]{:S(2)}, u32[]{:S(2)}) collective-permute-start(bf16[256,640]{1,0:T(8,128)(2,1)S(1)} %dynamic-slice_bitcast_fusion), channel_id=1, source_target_pairs={{0,1},{1,0},{2,3},{3,2},{4,5},{5,4},{6,7},{7,6},{8,9},{9,8},{10,11... | collective-permute-start | bytes 983048 | tf_op jit(solution)/shard_map/ppermute | solution.py:338
  130.9 0.7 copy-start.7
  138.1 13.2 %collective-permute-start.2 = (bf16[144,1152]{1,0:T(8,128)(2,1)S(1)}, bf16[144,1152]{1,0:T(8,128)(2,1)S(1)}, u32[]{:S(2)}, u32[]{:S(2)}) collective-permute-start(bf16[144,1152]{1,0:T(8,128)(2,1)S(1)} %get-tuple-element.19), channel_id=1, source_target_pairs={{0,32},{32,64},{64,96},{96,0},{128,160},{160,192},{192,224},{224,1... | collective-permute-start | bytes 995336 | tf_op jit(solution)/shard_map/ppermute | solution.py:319
  142.0 17.2 %collective-permute-start.3 = (bf16[144,1152]{1,0:T(8,128)(2,1)S(1)}, bf16[144,1152]{1,0:T(8,128)(2,1)S(1)}, u32[]{:S(2)}, u32[]{:S(2)}) collective-permute-start(bf16[144,1152]{1,0:T(8,128)(2,1)S(1)} %get-tuple-element.18), channel_id=1, source_target_pairs={{0,64},{32,96},{64,0},{96,32},{128,192},{160,224},{192,128},{224,1... | collective-permute-start | bytes 995336 | tf_op jit(solution)/shard_map/ppermute | solution.py:319
  146.0 14.9 %collective-permute-start.4 = (bf16[144,1152]{1,0:T(8,128)(2,1)S(1)}, bf16[144,1152]{1,0:T(8,128)(2,1)S(1)}, u32[]{:S(2)}, u32[]{:S(2)}) collective-permute-start(bf16[144,1152]{1,0:T(8,128)(2,1)S(1)} %get-tuple-element.17), channel_id=1, source_target_pairs={{0,96},{32,0},{64,32},{96,64},{128,224},{160,128},{192,160},{224,1... | collective-permute-start | bytes 995336 | tf_op jit(solution)/shard_map/ppermute | solution.py:319
  151.2 9.7 %copy-start.4 = (bf16[144,1152]{1,0:T(8,128)(2,1)}, bf16[144,1152]{1,0:T(8,128)(2,1)S(1)}, u32[]{:S(2)}) copy-start(bf16[144,1152]{1,0:T(8,128)(2,1)S(1)} %collective-permute-done.2.b_ref) | copy-start | bytes 995332
  159.2 1.7 copy-start.5
  160.9 0.7 copy-start.6
  165.6 16.6 %collective-permute-start.5 = (bf16[144,384]{1,0:T(8,128)(2,1)S(1)}, bf16[144,384]{1,0:T(8,128)(2,1)S(1)}, u32[]{:S(2)}, u32[]{:S(2)}) collective-permute-start(bf16[144,384]{1,0:T(8,128)(2,1)S(1)} %get-tuple-element.23), channel_id=1, source_target_pairs={{0,128},{32,160},{64,192},{96,224},{128,256},{160,288},{192,320},{... | collective-permute-start | bytes 331784 | tf_op jit(solution)/shard_map/ppermute | solution.py:325
  170.7 12.5 %collective-permute-start.6 = (bf16[144,384]{1,0:T(8,128)(2,1)S(1)}, bf16[144,384]{1,0:T(8,128)(2,1)S(1)}, u32[]{:S(2)}, u32[]{:S(2)}) collective-permute-start(bf16[144,384]{1,0:T(8,128)(2,1)S(1)} %get-tuple-element.22), channel_id=1, source_target_pairs={{0,256},{32,288},{64,320},{96,352},{128,384},{160,416},{192,448},{... | collective-permute-start | bytes 331784 | tf_op jit(solution)/shard_map/ppermute | solution.py:325
  176.7 10.7 %collective-permute-start.7 = (bf16[144,384]{1,0:T(8,128)(2,1)S(1)}, bf16[144,384]{1,0:T(8,128)(2,1)S(1)}, u32[]{:S(2)}, u32[]{:S(2)}) collective-permute-start(bf16[144,384]{1,0:T(8,128)(2,1)S(1)} %get-tuple-element.21), channel_id=1, source_target_pairs={{0,384},{32,416},{64,448},{96,480},{128,0},{160,32},{192,64},{224,... | collective-permute-start | bytes 331784 | tf_op jit(solution)/shard_map/ppermute | solution.py:325
  182.2 5.2 %copy-start.8 = (bf16[144,384]{1,0:T(8,128)(2,1)}, bf16[144,384]{1,0:T(8,128)(2,1)S(1)}, u32[]{:S(2)}) copy-start(bf16[144,384]{1,0:T(8,128)(2,1)S(1)} %collective-permute-done.5.b_ref) | copy-start | bytes 331780
  183.2 4.2 %copy-start.9 = (bf16[144,384]{1,0:T(8,128)(2,1)}, bf16[144,384]{1,0:T(8,128)(2,1)S(1)}, u32[]{:S(2)}) copy-start(bf16[144,384]{1,0:T(8,128)(2,1)S(1)} %collective-permute-done.6.c_ref) | copy-start | bytes 331780
  187.4 0.6 copy-start.10
  209.3 20.7 %all-to-all-start.3 = ((f32[16,32,128]{2,1,0:T(8,128)}), f32[16,32,128]{2,1,0:T(8,128)S(1)}, u32[]{:S(2)}, u32[]{:S(2)}) async-start(f32[16,32,128]{2,1,0:T(8,128)} %add_frames.1), calls=%async_computation.3 | async-start | bytes 524288 | tf_op jit(solution)/shard_map/all_to_all | solution.py:313
  230.0 0.7 copy-start.3
Sparse Core Ops, SparseCore 0:
  22.8 84.4 all-gather.3

commit v2 on v1

v2 whole, which is shorter than its diff:
```python
import jax
import jax.numpy as jnp
from jax import lax
from jax.experimental import pallas as pl
from jax.experimental.pallas import tpu as pltpu
from jax.sharding import PartitionSpec as P

HEADS = 16
HEAD_DIM = 72
WIDTH = 1152
FRAMES = 32
SLOTS = 8
TOKENS = FRAMES * SLOTS
ROWS = 36
QUARTER = ROWS // 4
HALF = 640
SCALE = 1.0 / HEAD_DIM**0.5
LANES = 128
TALL = 96
MIB = 1024 * 1024
NN = (((1,), (0,)), ((), ()))
NT = (((1,), (1,)), ((), ()))
TN = (((0,), (0,)), ((), ()))


def mm(a, b, dims):
    return lax.dot_general(a, b, dims, preferred_element_type=jnp.float32)


def window(head):
    first, last = head * HEAD_DIM, (head + 1) * HEAD_DIM - 1
    return first // LANES, last // LANES + 1


def head_mask(head):
    lo, hi = window(head)
    lane = lax.broadcasted_iota(jnp.int32, (1, (hi - lo) * LANES), 1) + lo * LANES
    own = (lane >= head * HEAD_DIM) & (lane < (head + 1) * HEAD_DIM)
    return jnp.where(own, 1.0, 0.0).astype(jnp.bfloat16)


def same_position():
    row = lax.broadcasted_iota(jnp.int32, (TOKENS, TOKENS), 0)
    col = lax.broadcasted_iota(jnp.int32, (TOKENS, TOKENS), 1)
    return jnp.where((row & (SLOTS - 1)) == (col & (SLOTS - 1)), 0.0, -1e30)


def as_tokens(x):
    return x.astype(jnp.float32).reshape(TOKENS, WIDTH).astype(jnp.bfloat16)


class Tiles:
    def __init__(self, store):
        self.open, self.store = {}, store

    def add(self, head, value):
        lo, hi = window(head)
        for tile in range(lo, hi):
            part = value[:, (tile - lo) * LANES : (tile - lo + 1) * LANES]
            self.open[tile] = self.open[tile] + part if tile in self.open else part
        keep = window(head + 1)[0] if head + 1 < HEADS else WIDTH // LANES
        for tile in sorted(self.open):
            if tile < keep:
                self.store(tile, self.open.pop(tile))


def pack_kernel(q_ref, k_ref, v_ref, dy_ref, out_ref, sems):
    copies = [
        pltpu.make_async_copy(ref, out_ref.at[:, i], sems.at[i])
        for i, ref in enumerate((q_ref, k_ref, v_ref, dy_ref))
    ]
    for copy in copies:
        copy.start()
    for copy in copies:
        copy.wait()


def pack(*arrays):
    return pl.pallas_call(
        pack_kernel,
        out_shape=jax.ShapeDtypeStruct((FRAMES, 4, SLOTS, WIDTH), jnp.bfloat16),
        in_specs=[pl.BlockSpec(memory_space=pl.ANY)] * 4,
        out_specs=pl.BlockSpec(memory_space=pltpu.VMEM),
        scratch_shapes=[pltpu.SemaphoreType.DMA((4,))],
        compiler_params=pltpu.CompilerParams(vmem_limit_bytes=60 * MIB),
        name="pack",
    )(*[a.reshape(FRAMES, SLOTS, WIDTH) for a in arrays])


def forward_kernel(
    place_ref, got_ref, order_ref, dy_out, own_out, other_out, stats_ref,
    raw_ref, pick_ref, q_ref, k_ref, v_ref, dy_ref, attn_ref, plain_ref, in_sems, out_sems,
):
    arrive = [pltpu.make_async_copy(got_ref.at[:, i], raw_ref.at[i], in_sems.at[i]) for i in range(4)]
    arrive.append(pltpu.make_async_copy(order_ref, pick_ref, in_sems.at[4]))
    for copy in arrive:
        copy.start()
    for i, ref in enumerate((q_ref, k_ref, v_ref, dy_ref)):
        arrive[i].wait()
        ref[...] = as_tokens(raw_ref[i])
    leave = [pltpu.make_async_copy(dy_ref, dy_out, out_sems.at[0])]
    leave[0].start()
    bias = same_position()

    def store(tile, value):
        plain_ref[:, tile * LANES : (tile + 1) * LANES] = value.astype(jnp.bfloat16)

    attn = Tiles(store)
    for head in range(HEADS):
        lo, hi = window(head)
        cols = slice(lo * LANES, hi * LANES)
        mask = head_mask(head)
        scores = mm(k_ref[:, cols] * mask, q_ref[:, cols], NT) * SCALE + bias
        top = jnp.max(scores, axis=0, keepdims=True)
        weight = jnp.exp(scores - top)
        inverse = 1.0 / jnp.sum(weight, axis=0, keepdims=True)
        stats_ref[head : head + 1, :] = top
        stats_ref[HEADS + head : HEADS + head + 1, :] = inverse
        attn.add(head, mm((weight * inverse).astype(jnp.bfloat16), v_ref[:, cols] * mask, TN))
    arrive[4].wait()
    for core in range(2):
        cols = slice(core * HALF, (core + 1) * HALF)
        attn_ref[core] = mm(plain_ref[...], pick_ref[:, cols], NN).astype(jnp.bfloat16)
    core = place_ref[0]
    leave.append(pltpu.make_async_copy(attn_ref.at[core], own_out, out_sems.at[1]))
    leave.append(pltpu.make_async_copy(attn_ref.at[1 - core], other_out, out_sems.at[2]))
    for copy in leave[1:]:
        copy.start()
    for copy in leave:
        copy.wait()


def selection():
    row = lax.broadcasted_iota(jnp.int32, (WIDTH, 2 * HALF), 0)
    col = lax.broadcasted_iota(jnp.int32, (WIDTH, 2 * HALF), 1)
    block, within = row // ROWS, row % ROWS
    place = (block % 2) * HALF + (within // QUARTER) * 144 + (block // 2) * QUARTER + within % QUARTER
    return (place == col).astype(jnp.bfloat16)


def forward(place, got, order):
    tokens = (TOKENS, WIDTH)
    halves = (2, TOKENS, HALF)
    return pl.pallas_call(
        forward_kernel,
        out_shape=(
            jax.ShapeDtypeStruct(tokens, jnp.bfloat16),
            jax.ShapeDtypeStruct((TOKENS, HALF), jnp.bfloat16),
            jax.ShapeDtypeStruct((TOKENS, HALF), jnp.bfloat16),
            jax.ShapeDtypeStruct((2 * HEADS, TOKENS), jnp.float32),
        ),
        in_specs=[pl.BlockSpec(memory_space=pltpu.SMEM)]
        + [pl.BlockSpec(memory_space=pl.ANY)] * 2,
        out_specs=[pl.BlockSpec(memory_space=pltpu.HBM)] * 3 + [pl.BlockSpec(memory_space=pltpu.VMEM)],
        scratch_shapes=[
            pltpu.VMEM((4, FRAMES, SLOTS, WIDTH), jnp.bfloat16),
            pltpu.VMEM((WIDTH, 2 * HALF), jnp.bfloat16),
            *[pltpu.VMEM(tokens, jnp.bfloat16)] * 4,
            pltpu.VMEM(halves, jnp.bfloat16),
            pltpu.VMEM(tokens, jnp.bfloat16),
            pltpu.SemaphoreType.DMA((5,)),
            pltpu.SemaphoreType.DMA((3,)),
        ],
        compiler_params=pltpu.CompilerParams(vmem_limit_bytes=48 * MIB),
        name="attention",
    )(place, got, order)


def backward_kernel(
    got_ref, dy_in, stats_ref, w_in, after_ref, out_hbm,
    raw_ref, q_ref, k_ref, v_ref, dy_ref, w_ref, ga_ref, across_ref, rows_ref, prob_ref, out_ref,
    sems, out_sems,
):
    arrive = [
        pltpu.make_async_copy(got_ref.at[:, i], raw_ref.at[i], sems.at[i]) for i in range(3)
    ]
    arrive.append(pltpu.make_async_copy(dy_in, dy_ref, sems.at[3]))
    for i in range(4):
        part = pl.ds(8 * i, 8)
        arrive.append(pltpu.make_async_copy(w_in.at[part], w_ref.at[part], sems.at[4 + i]))
    for i in (0, 1, 4, 5, 6, 7, 3, 2):
        arrive[i].start()
    bias = same_position()
    for i, ref in enumerate((q_ref, k_ref)):
        arrive[i].wait()
        ref[...] = as_tokens(raw_ref[i])
    for head in range(HEADS):
        lo, hi = window(head)
        cols = slice(lo * LANES, hi * LANES)
        scores = mm(k_ref[:, cols] * head_mask(head), q_ref[:, cols], NT) * SCALE + bias
        top = stats_ref[head : head + 1, :]
        inverse = stats_ref[HEADS + head : HEADS + head + 1, :]
        prob_ref[head] = jnp.exp(scores - top) * inverse
    for i in range(4):
        arrive[4 + i].wait()
        for block in range(8 * i, 8 * i + 8):
            rows_ref[block * ROWS : (block + 1) * ROWS, :] = w_ref[block]
    arrive[3].wait()
    for tile in range(WIDTH // LANES):
        cols = slice(tile * LANES, (tile + 1) * LANES)
        ga = mm(dy_ref[...], rows_ref[cols, :], NT)
        ga_ref[:, cols] = ga.astype(jnp.bfloat16)
        across_ref[cols, :] = ga.T.astype(jnp.bfloat16)
    arrive[2].wait()
    v_ref[...] = as_tokens(raw_ref[2])

    leave = []

    def storer(which, scale):
        def store(tile, value):
            if scale is not None:
                value = value * scale
            out_ref[:, which, :, tile * LANES : (tile + 1) * LANES] = value.reshape(
                FRAMES, SLOTS, LANES
            ).astype(jnp.bfloat16)
            if tile % 3 == 2:
                part = (slice(None), which, slice(None), pl.ds((tile - 2) * LANES, 3 * LANES))
                sem = out_sems.at[3 * which + tile // 3]
                leave.append(pltpu.make_async_copy(out_ref.at[part], out_hbm.at[part], sem))
                leave[-1].start()

        return store

    grad_q, grad_k = Tiles(storer(0, SCALE)), Tiles(storer(1, SCALE))
    grad_v = Tiles(storer(2, None))
    for head in range(HEADS):
        lo, hi = window(head)
        cols = slice(lo * LANES, hi * LANES)
        mask = head_mask(head)
        prob = prob_ref[head]
        grad_v.add(head, mm(prob.astype(jnp.bfloat16), ga_ref[:, cols] * mask, NN))
        product = prob * mm(v_ref[:, cols] * mask, across_ref[cols, :], NN)
        total = jnp.sum(product, axis=0, keepdims=True)
        grad_scores = (product - prob * total).astype(jnp.bfloat16)
        grad_k.add(head, mm(grad_scores, q_ref[:, cols] * mask, NN))
        grad_q.add(head, mm(grad_scores, k_ref[:, cols] * mask, TN))
    for copy in leave:
        copy.wait()


def backward(got, dy, stats, weight, after):
    tokens = pltpu.VMEM((TOKENS, WIDTH), jnp.bfloat16)
    return pl.pallas_call(
        backward_kernel,
        out_shape=pltpu.HBM((FRAMES, 3, SLOTS, WIDTH), jnp.bfloat16),
        in_specs=[
            pl.BlockSpec(memory_space=pl.ANY),
            pl.BlockSpec(memory_space=pl.ANY),
            pl.BlockSpec(memory_space=pltpu.VMEM),
            pl.BlockSpec(memory_space=pl.ANY),
            pl.BlockSpec(memory_space=pl.ANY),
        ],
        out_specs=pl.BlockSpec(memory_space=pltpu.HBM),
        scratch_shapes=[
            pltpu.VMEM((3, FRAMES, SLOTS, WIDTH), jnp.bfloat16),
            *[tokens] * 4,
            pltpu.VMEM((FRAMES, ROWS, WIDTH), jnp.bfloat16),
            tokens,
            pltpu.VMEM((WIDTH, TOKENS), jnp.bfloat16),
            pltpu.VMEM((WIDTH, WIDTH), jnp.bfloat16),
            pltpu.VMEM((HEADS, TOKENS, TOKENS), jnp.float32),
            pltpu.VMEM((FRAMES, 3, SLOTS, WIDTH), jnp.bfloat16),
            pltpu.SemaphoreType.DMA((8,)),
            pltpu.SemaphoreType.DMA((9,)),
        ],
        compiler_params=pltpu.CompilerParams(vmem_limit_bytes=52 * MIB),
        name="attention_gradients",
    )(got, dy, stats, weight, after)


def weight_kernel(
    attn_in, other_in, dy_in, dy_other_in, out_hbm, token_ref,
    attn_ref, other_ref, dy_ref, dy_other_ref, out_ref, sems, out_sems,
):
    pairs = (
        (attn_in, attn_ref),
        (dy_in, dy_ref),
        (other_in, other_ref),
        (dy_other_in, dy_other_ref),
    )
    arrive = [pltpu.make_async_copy(src, dst, sems.at[i]) for i, (src, dst) in enumerate(pairs)]
    for copy in arrive:
        copy.start()
    for copy in arrive:
        copy.wait()
    leave = []
    for tile in range(WIDTH // LANES):
        cols = slice(tile * LANES, (tile + 1) * LANES)
        total = mm(attn_ref[...], dy_ref[:, cols], TN)
        total += mm(other_ref[...], dy_other_ref[:, cols], TN)
        for x in range(4):
            out_ref[x, :, cols] = total[x * 144 : (x + 1) * 144].astype(jnp.bfloat16)
        if tile % 3 == 2:
            part = (slice(None), slice(None), pl.ds((tile - 2) * LANES, 3 * LANES))
            leave.append(
                pltpu.make_async_copy(out_ref.at[part], out_hbm.at[part], out_sems.at[tile // 3])
            )
            leave[-1].start()
    for copy in leave:
        copy.wait()
    token_ref[...] = jnp.zeros_like(token_ref)


def weight_term(attn, attn_in, dy, dy_in):
    half = pltpu.VMEM((TOKENS, HALF), jnp.bfloat16)
    tokens = pltpu.VMEM((TOKENS, WIDTH), jnp.bfloat16)
    return pl.pallas_call(
        weight_kernel,
        out_shape=(
            pltpu.HBM((4, 144, WIDTH), jnp.bfloat16),
            jax.ShapeDtypeStruct((8, LANES), jnp.float32),
        ),
        in_specs=[pl.BlockSpec(memory_space=pl.ANY)] * 4,
        out_specs=[pl.BlockSpec(memory_space=pltpu.HBM), pl.BlockSpec(memory_space=pltpu.VMEM)],
        scratch_shapes=[
            half,
            half,
            tokens,
            tokens,
            pltpu.VMEM((4, 144, WIDTH), jnp.bfloat16),
            pltpu.SemaphoreType.DMA((4,)),
            pltpu.SemaphoreType.DMA((3,)),
        ],
        compiler_params=pltpu.CompilerParams(vmem_limit_bytes=12 * MIB),
        name="weight_term",
    )(attn, attn_in, dy, dy_in)


def add_x_kernel(got_ref, out_ref):
    for tile in range(WIDTH // LANES):
        cols = slice(tile * LANES, (tile + 1) * LANES)
        parts = [got_ref[x, :, cols].astype(jnp.float32) for x in range(4)]
        total = (parts[0] + parts[1]) + (parts[2] + parts[3])
        out_ref[:, cols] = total.astype(jnp.bfloat16)


def add_x(got):
    return pl.pallas_call(
        add_x_kernel,
        out_shape=jax.ShapeDtypeStruct((144, WIDTH), jnp.bfloat16),
        in_specs=[pl.BlockSpec(memory_space=pltpu.VMEM)],
        out_specs=pl.BlockSpec(memory_space=pltpu.VMEM),
        compiler_params=pltpu.CompilerParams(vmem_limit_bytes=6 * MIB),
        name="add_x",
    )(got)


def add_z_kernel(a_ref, b_ref, out_ref, sum_ref):
    sum_ref[:, 9 * QUARTER :, :] = jnp.zeros((16, TALL - 9 * QUARTER, LANES), jnp.float32)
    for tile in range(WIDTH // LANES):
        cols = slice(tile * LANES, (tile + 1) * LANES)
        total = a_ref[:, cols].astype(jnp.float32) + b_ref[:, cols].astype(jnp.float32)
        for block in range(16):
            sum_ref[block, tile * QUARTER : (tile + 1) * QUARTER, :] = total[
                block * QUARTER : (block + 1) * QUARTER
            ]
    out_ref[...] = sum_ref[...].astype(jnp.bfloat16)


def add_z(a, b):
    return pl.pallas_call(
        add_z_kernel,
        out_shape=jax.ShapeDtypeStruct((16, TALL, LANES), jnp.bfloat16),
        in_specs=[pl.BlockSpec(memory_space=pltpu.VMEM)] * 2,
        out_specs=pl.BlockSpec(memory_space=pltpu.VMEM),
        scratch_shapes=[pltpu.VMEM((16, TALL, LANES), jnp.float32)],
        compiler_params=pltpu.CompilerParams(vmem_limit_bytes=6 * MIB),
        name="add_z",
    )(a, b)


def add_frames_kernel(got_ref, out_ref):
    total = got_ref[0].astype(jnp.float32)
    for i in range(1, 16):
        total += got_ref[i].astype(jnp.float32)
    for i in range(4):
        out_ref[i] = total


def add_frames(got):
    return pl.pallas_call(
        add_frames_kernel,
        out_shape=jax.ShapeDtypeStruct((4, TALL, LANES), jnp.float32),
        in_specs=[pl.BlockSpec(memory_space=pltpu.VMEM)],
        out_specs=pl.BlockSpec(memory_space=pltpu.VMEM),
        compiler_params=pltpu.CompilerParams(vmem_limit_bytes=4 * MIB),
        name="add_frames",
    )(got)


def assemble_kernel(got_ref, out_ref):
    for x in range(4):
        for tile in range(WIDTH // LANES):
            out_ref[x * QUARTER : (x + 1) * QUARTER, tile * LANES : (tile + 1) * LANES] = got_ref[
                x, tile * QUARTER : (tile + 1) * QUARTER, :
            ]


def assemble(got):
    return pl.pallas_call(
        assemble_kernel,
        out_shape=jax.ShapeDtypeStruct((ROWS, WIDTH), jnp.float32),
        in_specs=[pl.BlockSpec(memory_space=pltpu.VMEM)],
        out_specs=pl.BlockSpec(memory_space=pltpu.VMEM),
        compiler_params=pltpu.CompilerParams(vmem_limit_bytes=4 * MIB),
        name="assemble",
    )(got)


def at(y, z, core):
    return y * 4 + z * 2 + core


SWAP_CORE = [(i, i ^ 1) for i in range(FRAMES)]
SAME_CORE = [[at(y, z, c) for y in range(8) for z in range(2)] for c in range(2)]
ALONG_X = [[z * 4 + x for x in range(4)] for z in range(4)]


def all_to_all(x, axis, groups=None):
    return lax.all_to_all(
        x, axis, split_axis=0, concat_axis=0, tiled=True, axis_index_groups=groups
    )


def swap_z(x, bits):
    return lax.ppermute(x, "clip", [(z * 4 + i, (z ^ bits) * 4 + i) for z in range(4) for i in range(4)])


def on_device(queries, keys, values, grad_out, w_out):
    weight = lax.all_gather(w_out, "frame", axis=0)
    clip = lax.axis_index("clip")
    place = jnp.stack([lax.axis_index("frame") & 1, clip & 3, clip >> 2])
    got = all_to_all(pack(queries, keys, values, grad_out), "frame")
    dy, attn, other, stats = forward(place, got, selection())

    attn_in = lax.ppermute(other, "frame", SWAP_CORE)
    dy_in = lax.ppermute(dy, "frame", SWAP_CORE)
    term, token = weight_term(attn, attn_in, dy, dy_in)
    out = backward(got, dy, stats, weight, token)
    term = add_x(all_to_all(term, "clip", ALONG_X))
    out = all_to_all(out, "frame")
    pair = term.astype(jnp.float32) + swap_z(term, 1).astype(jnp.float32)
    pair = pair.astype(jnp.bfloat16)
    term = add_z(pair, swap_z(pair, 3))

    out, term = lax.optimization_barrier((out, term))
    term = add_frames(all_to_all(term, "frame", SAME_CORE))
    grad_weight = assemble(all_to_all(term, "clip", ALONG_X))
    shape = (1, 1, TOKENS, WIDTH)
    return (
        out[:, 0].reshape(shape),
        out[:, 1].reshape(shape),
        out[:, 2].reshape(shape),
        grad_weight,
    )


def solution(mesh):
    spread = P("clip", "frame", None, None)
    return jax.shard_map(
        on_device,
        mesh=mesh,
        in_specs=(spread, spread, spread, spread, P("frame", None)),
        out_specs=(spread, spread, spread, P("frame", None)),
        check_vma=False,
    )
```

time: 240 us -> 211 us (0.88)
  the two profiles are of different devices: /device:TPU:8 before, /device:TPU:2 now
where the time goes in v2:
time: 211 us; the launch traced here: 210 us
  waiting for transfers between devices  101 us (48%)
  starting transfers between devices  43.9 us (21%)
  Pallas kernels  23.3 us (11%)
  blocking collectives  20.5 us (10%)
  between operations  14.2 us (7%)
  other arithmetic  6.13 us (3%)
    all_to_all x4, waiting for transfers between devices, all_to_all(): lax.all_to_all(x, axis, split_axis=0, concat_axis=0, tiled=True, axis_ind...  64.9 us
    ppermute x2, waiting for transfers between devices, swap_z(): lax.ppermute(x, 'clip', [(z * 4 + i, (z ^ bits) * 4 + i) for z in range(4...  30.4 us
    all_to_all x4, starting transfers between devices, all_to_all(): lax.all_to_all(x, axis, split_axis=0, concat_axis=0, tiled=True, axis_ind...  23.5 us
    all_to_all x1, blocking collectives, all_to_all(): lax.all_to_all(x, axis, split_axis=0, concat_axis=0, tiled=True, axis_ind...  20.5 us
    ppermute x2, starting transfers between devices, swap_z(): lax.ppermute(x, 'clip', [(z * 4 + i, (z ^ bits) * 4 + i) for z in range(4...  16 us
    pallas_call x1, Pallas kernels, backward(): pl.pallas_call(backward_kernel, out_shape=pltpu.HBM((FRAMES, 3, SLOTS, WI...  10.5 us
    convert_element_type x1, other arithmetic, selection(): return (place == col).astype(jnp.bfloat16)  5.94 us
    pallas_call x1, Pallas kernels, forward(): pl.pallas_call(forward_kernel, out_shape=(jax.ShapeDtypeStruct(tokens, jn...  4.94 us
  transfers between devices with their start and end apart: 9, of which 7 were waited for; matrix products, arithmetic and copies ran while one was open for 4% of the time, Pallas kernels for 9%

profile of v2, /device:TPU:2, one launch (start us, length us, event | category | flops | bytes accessed | tf_op | source)
XLA Modules:
  0.0 210.2 jit_solution(10975586800180383296)
XLA Ops:
  7.2 3.1 %pack.1 = bf16[32,4,8,1152]{3,2,1,0:T(8,128)(2,1)} custom-call(bf16[32,8,1152]{2,1,0:T(8,128)(2,1)} %bitcast.14, bf16[32,8,1152]{2,1,0:T(8,128)(2,1)} %bitcast.15, bf16[32,8,1152]{2,1,0:T(8,128)(2,1)} %bitcast.16, bf16[32,8,1152]{2,1,0:T(8,128)(2,1)} %bitcast.17), custom_call_target="tpu_custom_call" | custom-call | tf_op jit(solution)/shard_map/pack/pallas_call | solution.py:79
  10.3 9.3 %all-to-all-start = ((bf16[32,4,8,1152]{3,2,1,0:T(8,128)(2,1)}), bf16[32,4,8,1152]{3,2,1,0:T(8,128)(2,1)S(1)}, u32[]{:S(2)}, u32[]{:S(2)}) async-start(bf16[32,4,8,1152]{3,2,1,0:T(8,128)(2,1)} %pack.1), calls=%async_computation | async-start | bytes 4718592 | tf_op jit(solution)/shard_map/all_to_all | solution.py:420
  20.5 5.9 %fusion.18.order_ref = bf16[1152,1280]{1,0:T(8,128)(2,1)} fusion(s32[1152]{0:T(1024)S(1)} %get-tuple-element.24, s32[1152]{0:T(1024)S(1)} %get-tuple-element.25, s32[1152]{0:T(1024)S(1)} %get-tuple-element.23, s32[1152]{0:T(1024)S(1)} %get-tuple-element.26, pred[1152]{0:T(1024)(128)(4,1)S(1)} %get-tuple-element.27, pred[1152]{0:T(1024)(128)(4,1)S(1)} %get-tuple-element.28), kind=kLoop, calls=%fused_computation.30 | loop fusion | flops 60456960 | bytes 2969856 | tf_op jit(solution)/shard_map/convert_element_type | solution.py:138
  26.4 58.2 %all-to-all-done.got_ref = bf16[32,4,8,1152]{3,2,1,0:T(8,128)(2,1)S(1)} async-done(((bf16[32,4,8,1152]{3,2,1,0:T(8,128)(2,1)}), bf16[32,4,8,1152]{3,2,1,0:T(8,128)(2,1)S(1)}, u32[]{:S(2)}, u32[]{:S(2)}) %all-to-all-start) | async-done | bytes 2359328 | tf_op jit(solution)/shard_map/all_to_all | solution.py:420
  84.7 4.9 %attention.1 = (bf16[256,1152]{1,0:T(8,128)(2,1)S(1)}, bf16[256,640]{1,0:T(8,128)(2,1)S(1)}, bf16[256,640]{1,0:T(8,128)(2,1)S(1)}, f32[32,256]{1,0:T(8,128)S(1)}) custom-call(s32[3]{0:T(128)S(1)} %pad_add_fusion.place_ref, bf16[32,4,8,1152]{3,2,1,0:T(8,128)(2,1)S(1)} %all-to-all-done.got_ref, bf16[1152,1280]{1,0:T(8,128)(2,1)} %fusion.18.order_ref), custom_call_target="tpu_custom_call" | custom-call | tf_op jit(solution)/shard_map/attention/pallas_call | solution.py:144
  89.6 1.9 collective-permute-start.1
  91.5 2.4 %collective-permute-start = (bf16[256,640]{1,0:T(8,128)(2,1)S(1)}, bf16[256,640]{1,0:T(8,128)(2,1)S(1)}, u32[]{:S(2)}, u32[]{:S(2)}) collective-permute-start(bf16[256,640]{1,0:T(8,128)(2,1)S(1)} %get-tuple-element.15), channel_id=1, source_target_pairs={{0,1},{1,0},{2,3},{3,2},{4,5},{5,4},{6,7},{7,6},{8,9},{9,8},{10,11... | collective-permute-start | bytes 983048 | tf_op jit(solution)/shard_map/ppermute | solution.py:436
  94.0 1.2 collective-permute-done.other_in
  95.2 3.0 %weight_term.1 = (bf16[4,144,1152]{2,1,0:T(8,128)(2,1)}, f32[8,128]{1,0:T(8,128)S(1)}) custom-call(bf16[256,640]{1,0:T(8,128)(2,1)S(1)} %get-tuple-element.14.attn_in, bf16[256,640]{1,0:T(8,128)(2,1)S(1)} %collective-permute-done.other_in, bf16[256,1152]{1,0:T(8,128)(2,1)S(1)} %get-tuple-element.12.dy_in, ...), custom_call_target="tpu_custom_call" | custom-call | tf_op jit(solution)/shard_map/weight_term/pallas_call | solution.py:307
  98.2 5.4 %all-to-all-start.2 = ((bf16[4,144,1152]{2,1,0:T(8,128)(2,1)}), bf16[4,144,1152]{2,1,0:T(8,128)(2,1)S(1)}, u32[]{:S(2)}, u32[]{:S(2)}) async-start(bf16[4,144,1152]{2,1,0:T(8,128)(2,1)} %get-tuple-element.17), calls=%async_computation.2 | async-start | bytes 2654208 | tf_op jit(solution)/shard_map/all_to_all | solution.py:420
  103.6 3.7 %all-gather.4.cloned.1.call-done.w_in = bf16[32,36,1152]{2,1,0:T(8,128)(2,1)} async-done(((bf16[1,36,1152]{2,1,0:T(8,128)(2,1)}), bf16[32,36,1152]{2,1,0:T(8,128)(2,1)}) %all-gather.4.cloned.1.call-update) | async-done | bytes 2654224 | tf_op jit(solution)/shard_map/all_gather | solution.py:430
  107.3 10.5 %attention_gradients.1 = bf16[32,3,8,1152]{3,2,1,0:T(8,128)(2,1)} custom-call(bf16[32,4,8,1152]{3,2,1,0:T(8,128)(2,1)} %copy-done, bf16[256,1152]{1,0:T(8,128)(2,1)S(1)} %get-tuple-element.12.dy_in, f32[32,256]{1,0:T(8,128)S(1)} %get-tuple-element.13.stats_ref, bf16[32,36,1152]{2,1,0:T(8,128)(2,1)} %all-gather.4.cloned.1.call-done.w_in, ...), custom_call_target="tpu_custom_call" | custom-call | tf_op jit(solution)/shard_map/attention_gradients/pallas_call | solution.py:243
  117.8 3.0 %all-to-all-done.2.got_ref = bf16[4,144,1152]{2,1,0:T(8,128)(2,1)S(1)} async-done(((bf16[4,144,1152]{2,1,0:T(8,128)(2,1)}), bf16[4,144,1152]{2,1,0:T(8,128)(2,1)S(1)}, u32[]{:S(2)}, u32[]{:S(2)}) %all-to-all-start.2) | async-done | bytes 1327136 | tf_op jit(solution)/shard_map/all_to_all | solution.py:420
  120.8 4.0 %all-to-all-start.1 = ((bf16[32,3,8,1152]{3,2,1,0:T(8,128)(2,1)}), bf16[32,3,8,1152]{3,2,1,0:T(8,128)(2,1)S(1)}, u32[]{:S(2)}, u32[]{:S(2)}) async-start(bf16[32,3,8,1152]{3,2,1,0:T(8,128)(2,1)} %attention_gradients.1), calls=%async_computation.1 | async-start | bytes 3538944 | tf_op jit(solution)/shard_map/all_to_all | solution.py:420
  125.0 6.5 %collective-permute-start.2 = (bf16[144,1152]{1,0:T(8,128)(2,1)S(1)}, bf16[144,1152]{1,0:T(8,128)(2,1)S(1)}, u32[]{:S(2)}, u32[]{:S(2)}) collective-permute-start(bf16[144,1152]{1,0:T(8,128)(2,1)S(1)} %add_x.1), channel_id=1, source_target_pairs={{0,128},{32,160},{64,192},{96,224},{128,0},{160,32},{192,64},{224,... | collective-permute-start | bytes 995336 | tf_op jit(solution)/shard_map/ppermute | solution.py:426
  131.6 15.6 %collective-permute-done.2 = bf16[144,1152]{1,0:T(8,128)(2,1)S(1)} collective-permute-done((bf16[144,1152]{1,0:T(8,128)(2,1)S(1)}, bf16[144,1152]{1,0:T(8,128)(2,1)S(1)}, u32[]{:S(2)}, u32[]{:S(2)}) %collective-permute-start.2) | collective-permute-done | bytes 331808 | tf_op jit(solution)/shard_map/ppermute | solution.py:426
  147.2 9.5 %collective-permute-start.3 = (bf16[144,1152]{1,0:T(8,128)(2,1)S(1)}, bf16[144,1152]{1,0:T(8,128)(2,1)S(1)}, u32[]{:S(2)}, u32[]{:S(2)}) collective-permute-start(bf16[144,1152]{1,0:T(8,128)(2,1)S(1)} %add_convert_fusion.a_ref), channel_id=1, source_target_pairs={{0,384},{32,416},{64,448},{96,480},{128,256},{160,288},{192,320},{... | collective-permute-start | bytes 995336 | tf_op jit(solution)/shard_map/ppermute | solution.py:426
  156.7 14.9 %collective-permute-done.3.b_ref = bf16[144,1152]{1,0:T(8,128)(2,1)S(1)} collective-permute-done((bf16[144,1152]{1,0:T(8,128)(2,1)S(1)}, bf16[144,1152]{1,0:T(8,128)(2,1)S(1)}, u32[]{:S(2)}, u32[]{:S(2)}) %collective-permute-start.3) | collective-permute-done | bytes 331808 | tf_op jit(solution)/shard_map/ppermute | solution.py:426
  171.8 20.5 %all_to_all.25.got_ref = bf16[16,96,128]{2,1,0:T(8,128)(2,1)S(1)} all-to-all(bf16[16,96,128]{2,1,0:T(8,128)(2,1)S(1)} %add_z.1), channel_id=1, replica_groups={{0,2,4,6,8,10,12,14,16,18,20,22,24,26,28,30},{1,3,5,7,9,11,13,15,17,19,..., dimensions={0} | all-to-all | bytes 786432 | tf_op jit(solution)/shard_map/all_to_all | solution.py:420
  192.2 0.7 add_frames.1
  193.0 4.8 %all-to-all-start.4 = ((f32[4,96,128]{2,1,0:T(8,128)}), f32[4,96,128]{2,1,0:T(8,128)S(1)}, u32[]{:S(2)}, u32[]{:S(2)}) async-start(f32[4,96,128]{2,1,0:T(8,128)} %add_frames.1), calls=%async_computation.4 | async-start | bytes 393216 | tf_op jit(solution)/shard_map/all_to_all | solution.py:420
  197.7 1.2 slice_bitcast_fusion
  199.0 3.6 %all-to-all-done.4.got_ref = f32[4,96,128]{2,1,0:T(8,128)S(1)} async-done(((f32[4,96,128]{2,1,0:T(8,128)}), f32[4,96,128]{2,1,0:T(8,128)S(1)}, u32[]{:S(2)}, u32[]{:S(2)}) %all-to-all-start.4) | async-done | bytes 196640 | tf_op jit(solution)/shard_map/all_to_all | solution.py:420
  202.6 0.7 assemble.1
  (13 shorter events, 1.2 us)
Async XLA Ops:
  10.3 74.4 %all-to-all-start = ((bf16[32,4,8,1152]{3,2,1,0:T(8,128)(2,1)}), bf16[32,4,8,1152]{3,2,1,0:T(8,128)(2,1)S(1)}, u32[]{:S(2)}, u32[]{:S(2)}) async-start(bf16[32,4,8,1152]{3,2,1,0:T(8,128)(2,1)} %pack.1), calls=%async_computation | async-start | bytes 4718592 | tf_op jit(solution)/shard_map/all_to_all | solution.py:420
  19.6 87.7 %all-gather.4.cloned.1.call-start = ((), (), s32[]{:S(2)}) async-start(), calls=%async_computation.5 | async-start | bytes 3041280 | tf_op jit(solution)/shard_map/all_gather | solution.py:430
  84.7 13.6 %copy-start = (bf16[32,4,8,1152]{3,2,1,0:T(8,128)(2,1)}, bf16[32,4,8,1152]{3,2,1,0:T(8,128)(2,1)S(1)}, u32[]{:S(2)}) copy-start(bf16[32,4,8,1152]{3,2,1,0:T(8,128)(2,1)S(1)} %all-to-all-done.got_ref) | copy-start | bytes 7077892
  89.6 5.6 %collective-permute-start.1 = (bf16[256,1152]{1,0:T(8,128)(2,1)S(1)}, bf16[256,1152]{1,0:T(8,128)(2,1)S(1)}, u32[]{:S(2)}, u32[]{:S(2)}) collective-permute-start(bf16[256,1152]{1,0:T(8,128)(2,1)S(1)} %get-tuple-element.12.dy_in), channel_id=1, source_target_pairs={{0,1},{1,0},{2,3},{3,2},{4,5},{5,4},{6,7},{7,6},{8,9},{9,8},{10,11... | collective-permute-start | bytes 1769480 | tf_op jit(solution)/shard_map/ppermute | solution.py:437
  91.5 3.6 %collective-permute-start = (bf16[256,640]{1,0:T(8,128)(2,1)S(1)}, bf16[256,640]{1,0:T(8,128)(2,1)S(1)}, u32[]{:S(2)}, u32[]{:S(2)}) collective-permute-start(bf16[256,640]{1,0:T(8,128)(2,1)S(1)} %get-tuple-element.15), channel_id=1, source_target_pairs={{0,1},{1,0},{2,3},{3,2},{4,5},{5,4},{6,7},{7,6},{8,9},{9,8},{10,11... | collective-permute-start | bytes 983048 | tf_op jit(solution)/shard_map/ppermute | solution.py:436
  98.2 22.6 %all-to-all-start.2 = ((bf16[4,144,1152]{2,1,0:T(8,128)(2,1)}), bf16[4,144,1152]{2,1,0:T(8,128)(2,1)S(1)}, u32[]{:S(2)}, u32[]{:S(2)}) async-start(bf16[4,144,1152]{2,1,0:T(8,128)(2,1)} %get-tuple-element.17), calls=%async_computation.2 | async-start | bytes 2654208 | tf_op jit(solution)/shard_map/all_to_all | solution.py:420
  120.8 51.0 %all-to-all-start.1 = ((bf16[32,3,8,1152]{3,2,1,0:T(8,128)(2,1)}), bf16[32,3,8,1152]{3,2,1,0:T(8,128)(2,1)S(1)}, u32[]{:S(2)}, u32[]{:S(2)}) async-start(bf16[32,3,8,1152]{3,2,1,0:T(8,128)(2,1)} %attention_gradients.1), calls=%async_computation.1 | async-start | bytes 3538944 | tf_op jit(solution)/shard_map/all_to_all | solution.py:420
  125.0 22.1 %collective-permute-start.2 = (bf16[144,1152]{1,0:T(8,128)(2,1)S(1)}, bf16[144,1152]{1,0:T(8,128)(2,1)S(1)}, u32[]{:S(2)}, u32[]{:S(2)}) collective-permute-start(bf16[144,1152]{1,0:T(8,128)(2,1)S(1)} %add_x.1), channel_id=1, source_target_pairs={{0,128},{32,160},{64,192},{96,224},{128,0},{160,32},{192,64},{224,... | collective-permute-start | bytes 995336 | tf_op jit(solution)/shard_map/ppermute | solution.py:426
  147.2 24.4 %collective-permute-start.3 = (bf16[144,1152]{1,0:T(8,128)(2,1)S(1)}, bf16[144,1152]{1,0:T(8,128)(2,1)S(1)}, u32[]{:S(2)}, u32[]{:S(2)}) collective-permute-start(bf16[144,1152]{1,0:T(8,128)(2,1)S(1)} %add_convert_fusion.a_ref), channel_id=1, source_target_pairs={{0,384},{32,416},{64,448},{96,480},{128,256},{160,288},{192,320},{... | collective-permute-start | bytes 995336 | tf_op jit(solution)/shard_map/ppermute | solution.py:426
  193.0 9.7 %all-to-all-start.4 = ((f32[4,96,128]{2,1,0:T(8,128)}), f32[4,96,128]{2,1,0:T(8,128)S(1)}, u32[]{:S(2)}, u32[]{:S(2)}) async-start(f32[4,96,128]{2,1,0:T(8,128)} %add_frames.1), calls=%async_computation.4 | async-start | bytes 393216 | tf_op jit(solution)/shard_map/all_to_all | solution.py:420
Sparse Core Ops, SparseCore 0:
  22.6 84.6 all-gather.3

commit v3 on v2

--- a/solution.py
+++ b/solution.py
@@ -88,18 +88,19 @@
 
 
 def forward_kernel(
-    place_ref, got_ref, order_ref, dy_out, own_out, other_out, stats_ref,
-    raw_ref, pick_ref, q_ref, k_ref, v_ref, dy_ref, attn_ref, plain_ref, in_sems, out_sems,
+    place_ref, got_ref, order_ref, dy_out, own_out, send_out, stats_ref,
+    pick_ref, q_ref, k_ref, v_ref, dy_ref, attn_ref, plain_ref, in_sem, out_sems,
 ):
-    arrive = [pltpu.make_async_copy(got_ref.at[:, i], raw_ref.at[i], in_sems.at[i]) for i in range(4)]
-    arrive.append(pltpu.make_async_copy(order_ref, pick_ref, in_sems.at[4]))
-    for copy in arrive:
+    arrive = pltpu.make_async_copy(order_ref, pick_ref, in_sem)
+    arrive.start()
+    for i, ref in enumerate((q_ref, k_ref, v_ref, dy_ref)):
+        ref[...] = as_tokens(got_ref[:, i])
+    leave = [
+        pltpu.make_async_copy(dy_ref, dy_out, out_sems.at[0]),
+        pltpu.make_async_copy(dy_ref, send_out.at[:, pl.ds(HALF, WIDTH)], out_sems.at[3]),
+    ]
+    for copy in leave:
         copy.start()
-    for i, ref in enumerate((q_ref, k_ref, v_ref, dy_ref)):
-        arrive[i].wait()
-        ref[...] = as_tokens(raw_ref[i])
-    leave = [pltpu.make_async_copy(dy_ref, dy_out, out_sems.at[0])]
-    leave[0].start()
     bias = same_position()
 
     def store(tile, value):
@@ -117,14 +118,16 @@
         stats_ref[head : head + 1, :] = top
         stats_ref[HEADS + head : HEADS + head + 1, :] = inverse
         attn.add(head, mm((weight * inverse).astype(jnp.bfloat16), v_ref[:, cols] * mask, TN))
-    arrive[4].wait()
+    arrive.wait()
     for core in range(2):
         cols = slice(core * HALF, (core + 1) * HALF)
         attn_ref[core] = mm(plain_ref[...], pick_ref[:, cols], NN).astype(jnp.bfloat16)
     core = place_ref[0]
     leave.append(pltpu.make_async_copy(attn_ref.at[core], own_out, out_sems.at[1]))
-    leave.append(pltpu.make_async_copy(attn_ref.at[1 - core], other_out, out_sems.at[2]))
-    for copy in leave[1:]:
+    leave.append(
+        pltpu.make_async_copy(attn_ref.at[1 - core], send_out.at[:, pl.ds(0, HALF)], out_sems.at[2])
+    )
+    for copy in leave[2:]:
         copy.start()
     for copy in leave:
         copy.wait()
@@ -146,20 +149,19 @@
         out_shape=(
             jax.ShapeDtypeStruct(tokens, jnp.bfloat16),
             jax.ShapeDtypeStruct((TOKENS, HALF), jnp.bfloat16),
-            jax.ShapeDtypeStruct((TOKENS, HALF), jnp.bfloat16),
+            jax.ShapeDtypeStruct((TOKENS, HALF + WIDTH), jnp.bfloat16),
             jax.ShapeDtypeStruct((2 * HEADS, TOKENS), jnp.float32),
         ),
         in_specs=[pl.BlockSpec(memory_space=pltpu.SMEM)]
-        + [pl.BlockSpec(memory_space=pl.ANY)] * 2,
+        + [pl.BlockSpec(memory_space=pltpu.VMEM), pl.BlockSpec(memory_space=pl.ANY)],
         out_specs=[pl.BlockSpec(memory_space=pltpu.HBM)] * 3 + [pl.BlockSpec(memory_space=pltpu.VMEM)],
         scratch_shapes=[
-            pltpu.VMEM((4, FRAMES, SLOTS, WIDTH), jnp.bfloat16),
             pltpu.VMEM((WIDTH, 2 * HALF), jnp.bfloat16),
             *[pltpu.VMEM(tokens, jnp.bfloat16)] * 4,
             pltpu.VMEM(halves, jnp.bfloat16),
             pltpu.VMEM(tokens, jnp.bfloat16),
-            pltpu.SemaphoreType.DMA((5,)),
-            pltpu.SemaphoreType.DMA((3,)),
+            pltpu.SemaphoreType.DMA,
+            pltpu.SemaphoreType.DMA((4,)),
         ],
         compiler_params=pltpu.CompilerParams(vmem_limit_bytes=48 * MIB),
         name="attention",
@@ -269,14 +271,14 @@
 
 
 def weight_kernel(
-    attn_in, other_in, dy_in, dy_other_in, out_hbm, token_ref,
+    attn_in, dy_in, other_in, out_hbm, token_ref,
     attn_ref, other_ref, dy_ref, dy_other_ref, out_ref, sems, out_sems,
 ):
     pairs = (
         (attn_in, attn_ref),
         (dy_in, dy_ref),
-        (other_in, other_ref),
-        (dy_other_in, dy_other_ref),
+        (other_in.at[:, pl.ds(0, HALF)], other_ref),
+        (other_in.at[:, pl.ds(HALF, WIDTH)], dy_other_ref),
     )
     arrive = [pltpu.make_async_copy(src, dst, sems.at[i]) for i, (src, dst) in enumerate(pairs)]
     for copy in arrive:
@@ -301,7 +303,7 @@
     token_ref[...] = jnp.zeros_like(token_ref)
 
 
-def weight_term(attn, attn_in, dy, dy_in):
+def weight_term(attn, dy, other):
     half = pltpu.VMEM((TOKENS, HALF), jnp.bfloat16)
     tokens = pltpu.VMEM((TOKENS, WIDTH), jnp.bfloat16)
     return pl.pallas_call(
@@ -310,7 +312,7 @@
             pltpu.HBM((4, 144, WIDTH), jnp.bfloat16),
             jax.ShapeDtypeStruct((8, LANES), jnp.float32),
         ),
-        in_specs=[pl.BlockSpec(memory_space=pl.ANY)] * 4,
+        in_specs=[pl.BlockSpec(memory_space=pl.ANY)] * 3,
         out_specs=[pl.BlockSpec(memory_space=pltpu.HBM), pl.BlockSpec(memory_space=pltpu.VMEM)],
         scratch_shapes=[
             half,
@@ -323,7 +325,7 @@
         ],
         compiler_params=pltpu.CompilerParams(vmem_limit_bytes=12 * MIB),
         name="weight_term",
-    )(attn, attn_in, dy, dy_in)
+    )(attn, dy, other)
 
 
 def add_x_kernel(got_ref, out_ref):
@@ -431,11 +433,10 @@
     clip = lax.axis_index("clip")
     place = jnp.stack([lax.axis_index("frame") & 1, clip & 3, clip >> 2])
     got = all_to_all(pack(queries, keys, values, grad_out), "frame")
-    dy, attn, other, stats = forward(place, got, selection())
-
-    attn_in = lax.ppermute(other, "frame", SWAP_CORE)
-    dy_in = lax.ppermute(dy, "frame", SWAP_CORE)
-    term, token = weight_term(attn, attn_in, dy, dy_in)
+    dy, attn, send, stats = forward(place, got, selection())
+
+    other = lax.ppermute(send, "frame", SWAP_CORE)
+    term, token = weight_term(attn, dy, other)
     out = backward(got, dy, stats, weight, token)
     term = add_x(all_to_all(term, "clip", ALONG_X))
     out = all_to_all(out, "frame")

time: 211 us -> 210 us (level)
  starting transfers between devices: 43.9 us -> 41.7 us
    all_to_all x4, waiting for transfers between devices: 64.9 us -> 61.6 us  [all_to_all(): lax.all_to_all(x, axis, split_axis=0, concat_axis=0, tiled=True, axis_ind...]
    ppermute x2 -> x1, starting transfers between devices: 4.33 us -> 1.92 us  [on_device(): other = lax.ppermute(send, 'frame', SWAP_CORE)]
  transfers between devices with their start and end apart: 9 -> 8, of which waited for: 7 -> 7; matrix products, arithmetic and copies ran while one was open for 4% -> 4% of each run, Pallas kernels for 9% -> 9%
where the time goes in v3:
time: 210 us; the launch traced here: 209 us
  waiting for transfers between devices  101 us (48%)
  starting transfers between devices  41.7 us (20%)
  Pallas kernels  23 us (11%)
  blocking collectives  20.3 us (10%)
  between operations  14.2 us (7%)
  other arithmetic  6.18 us (3%)
  local copies, waits for them, and re-layouts  2.67 us (1%)
    all_to_all x4, waiting for transfers between devices, all_to_all(): lax.all_to_all(x, axis, split_axis=0, concat_axis=0, tiled=True, axis_ind...  61.6 us
    ppermute x2, waiting for transfers between devices, swap_z(): lax.ppermute(x, 'clip', [(z * 4 + i, (z ^ bits) * 4 + i) for z in range(4...  31.1 us
    all_to_all x4, starting transfers between devices, all_to_all(): lax.all_to_all(x, axis, split_axis=0, concat_axis=0, tiled=True, axis_ind...  25.4 us
    all_to_all x1, blocking collectives, all_to_all(): lax.all_to_all(x, axis, split_axis=0, concat_axis=0, tiled=True, axis_ind...  20.3 us
    ppermute x2, starting transfers between devices, swap_z(): lax.ppermute(x, 'clip', [(z * 4 + i, (z ^ bits) * 4 + i) for z in range(4...  14.4 us
    pallas_call x1, Pallas kernels, backward(): pl.pallas_call(backward_kernel, out_shape=pltpu.HBM((FRAMES, 3, SLOTS, WI...  10.5 us
    convert_element_type x1, other arithmetic, selection(): return (place == col).astype(jnp.bfloat16)  6 us
    all_gather x1, waiting for transfers between devices, on_device(): weight = lax.all_gather(w_out, 'frame', axis=0)  5.26 us
  transfers between devices with their start and end apart: 8, of which 7 were waited for; matrix products, arithmetic and copies ran while one was open for 4% of the time, Pallas kernels for 9%

profile of v3, /device:TPU:2, one launch (start us, length us, event | category | flops | bytes accessed | tf_op | source)
XLA Modules:
  0.0 209.2 jit_solution(14476785932791475946)
XLA Ops:
  7.2 3.1 %pack.1 = bf16[32,4,8,1152]{3,2,1,0:T(8,128)(2,1)} custom-call(bf16[32,8,1152]{2,1,0:T(8,128)(2,1)} %bitcast.14, bf16[32,8,1152]{2,1,0:T(8,128)(2,1)} %bitcast.15, bf16[32,8,1152]{2,1,0:T(8,128)(2,1)} %bitcast.16, bf16[32,8,1152]{2,1,0:T(8,128)(2,1)} %bitcast.17), custom_call_target="tpu_custom_call" | custom-call | tf_op jit(solution)/shard_map/pack/pallas_call | solution.py:79
  10.3 9.3 %all-to-all-start = ((bf16[32,4,8,1152]{3,2,1,0:T(8,128)(2,1)}), bf16[32,4,8,1152]{3,2,1,0:T(8,128)(2,1)S(1)}, u32[]{:S(2)}, u32[]{:S(2)}) async-start(bf16[32,4,8,1152]{3,2,1,0:T(8,128)(2,1)} %pack.1), calls=%async_computation | async-start | bytes 4718592 | tf_op jit(solution)/shard_map/all_to_all | solution.py:422
  19.7 0.7 all-gather.4.cloned.1.call-update
  20.4 6.0 %fusion.18.order_ref = bf16[1152,1280]{1,0:T(8,128)(2,1)} fusion(s32[1152]{0:T(1024)S(1)} %get-tuple-element.24, s32[1152]{0:T(1024)S(1)} %get-tuple-element.25, s32[1152]{0:T(1024)S(1)} %get-tuple-element.23, s32[1152]{0:T(1024)S(1)} %get-tuple-element.26, pred[1152]{0:T(1024)(128)(4,1)S(1)} %get-tuple-element.27, pred[1152]{0:T(1024)(128)(4,1)S(1)} %get-tuple-element.28), kind=kLoop, calls=%fused_computation.30 | loop fusion | flops 60456960 | bytes 2969856 | tf_op jit(solution)/shard_map/convert_element_type | solution.py:141
  26.5 58.2 %all-to-all-done.got_ref = bf16[32,4,8,1152]{3,2,1,0:T(8,128)(2,1)S(1)} async-done(((bf16[32,4,8,1152]{3,2,1,0:T(8,128)(2,1)}), bf16[32,4,8,1152]{3,2,1,0:T(8,128)(2,1)S(1)}, u32[]{:S(2)}, u32[]{:S(2)}) %all-to-all-start) | async-done | bytes 2359328 | tf_op jit(solution)/shard_map/all_to_all | solution.py:422
  84.7 4.7 %attention.1 = (bf16[256,1152]{1,0:T(8,128)(2,1)S(1)}, bf16[256,640]{1,0:T(8,128)(2,1)S(1)}, bf16[256,1792]{1,0:T(8,128)(2,1)S(1)}, f32[32,256]{1,0:T(8,128)S(1)}) custom-call(s32[3]{0:T(128)S(1)} %pad_add_fusion.place_ref, bf16[32,4,8,1152]{3,2,1,0:T(8,128)(2,1)S(1)} %all-to-all-done.got_ref, bf16[1152,1280]{1,0:T(8,128)(2,1)} %fusion.18.order_ref), custom_call_target="tpu_custom_call" | custom-call | tf_op jit(solution)/shard_map/attention/pallas_call | solution.py:147
  89.4 1.9 collective-permute-start
  91.3 2.4 %collective-permute-done.other_in = bf16[256,1792]{1,0:T(8,128)(2,1)S(1)} collective-permute-done((bf16[256,1792]{1,0:T(8,128)(2,1)S(1)}, bf16[256,1792]{1,0:T(8,128)(2,1)S(1)}, u32[]{:S(2)}, u32[]{:S(2)}) %collective-permute-start) | collective-permute-done | bytes 917536 | tf_op jit(solution)/shard_map/ppermute | solution.py:438
  93.8 2.9 %weight_term.1 = (bf16[4,144,1152]{2,1,0:T(8,128)(2,1)}, f32[8,128]{1,0:T(8,128)S(1)}) custom-call(bf16[256,640]{1,0:T(8,128)(2,1)S(1)} %get-tuple-element.14.attn_in, bf16[256,1152]{1,0:T(8,128)(2,1)S(1)} %get-tuple-element.12.dy_in, bf16[256,1792]{1,0:T(8,128)(2,1)S(1)} %collective-permute-done.other_in), custom_call_target="tpu_custom_call" | custom-call | tf_op jit(solution)/shard_map/weight_term/pallas_call | solution.py:309
  96.7 5.4 %all-to-all-start.2 = ((bf16[4,144,1152]{2,1,0:T(8,128)(2,1)}), bf16[4,144,1152]{2,1,0:T(8,128)(2,1)S(1)}, u32[]{:S(2)}, u32[]{:S(2)}) async-start(bf16[4,144,1152]{2,1,0:T(8,128)(2,1)} %get-tuple-element.17), calls=%async_computation.2 | async-start | bytes 2654208 | tf_op jit(solution)/shard_map/all_to_all | solution.py:422
  102.1 5.3 %all-gather.4.cloned.1.call-done.w_in = bf16[32,36,1152]{2,1,0:T(8,128)(2,1)} async-done(((bf16[1,36,1152]{2,1,0:T(8,128)(2,1)}), bf16[32,36,1152]{2,1,0:T(8,128)(2,1)}) %all-gather.4.cloned.1.call-update) | async-done | bytes 2654224 | tf_op jit(solution)/shard_map/all_gather | solution.py:432
  107.3 10.5 %attention_gradients.1 = bf16[32,3,8,1152]{3,2,1,0:T(8,128)(2,1)} custom-call(bf16[32,4,8,1152]{3,2,1,0:T(8,128)(2,1)} %copy-done, bf16[256,1152]{1,0:T(8,128)(2,1)S(1)} %get-tuple-element.12.dy_in, f32[32,256]{1,0:T(8,128)S(1)} %get-tuple-element.13.stats_ref, bf16[32,36,1152]{2,1,0:T(8,128)(2,1)} %all-gather.4.cloned.1.call-done.w_in, ...), custom_call_target="tpu_custom_call" | custom-call | tf_op jit(solution)/shard_map/attention_gradients/pallas_call | solution.py:245
  117.8 1.2 all-to-all-done.2.got_ref
  119.0 5.9 %all-to-all-start.1 = ((bf16[32,3,8,1152]{3,2,1,0:T(8,128)(2,1)}), bf16[32,3,8,1152]{3,2,1,0:T(8,128)(2,1)}, u32[]{:S(2)}, u32[]{:S(2)}) async-start(bf16[32,3,8,1152]{3,2,1,0:T(8,128)(2,1)} %attention_gradients.1), calls=%async_computation.1 | async-start | bytes 3538944 | tf_op jit(solution)/shard_map/all_to_all | solution.py:422
  125.1 5.4 %collective-permute-start.1 = (bf16[144,1152]{1,0:T(8,128)(2,1)S(1)}, bf16[144,1152]{1,0:T(8,128)(2,1)S(1)}, u32[]{:S(2)}, u32[]{:S(2)}) collective-permute-start(bf16[144,1152]{1,0:T(8,128)(2,1)S(1)} %add_x.1), channel_id=1, source_target_pairs={{0,128},{32,160},{64,192},{96,224},{128,0},{160,32},{192,64},{224,... | collective-permute-start | bytes 995336 | tf_op jit(solution)/shard_map/ppermute | solution.py:428
  130.5 16.0 %collective-permute-done.1 = bf16[144,1152]{1,0:T(8,128)(2,1)S(1)} collective-permute-done((bf16[144,1152]{1,0:T(8,128)(2,1)S(1)}, bf16[144,1152]{1,0:T(8,128)(2,1)S(1)}, u32[]{:S(2)}, u32[]{:S(2)}) %collective-permute-start.1) | collective-permute-done | bytes 331808 | tf_op jit(solution)/shard_map/ppermute | solution.py:428
  146.6 9.0 %collective-permute-start.2 = (bf16[144,1152]{1,0:T(8,128)(2,1)S(1)}, bf16[144,1152]{1,0:T(8,128)(2,1)S(1)}, u32[]{:S(2)}, u32[]{:S(2)}) collective-permute-start(bf16[144,1152]{1,0:T(8,128)(2,1)S(1)} %add_convert_fusion.a_ref), channel_id=1, source_target_pairs={{0,384},{32,416},{64,448},{96,480},{128,256},{160,288},{192,320},{... | collective-permute-start | bytes 995336 | tf_op jit(solution)/shard_map/ppermute | solution.py:428
  155.6 15.1 %collective-permute-done.2.b_ref = bf16[144,1152]{1,0:T(8,128)(2,1)S(1)} collective-permute-done((bf16[144,1152]{1,0:T(8,128)(2,1)S(1)}, bf16[144,1152]{1,0:T(8,128)(2,1)S(1)}, u32[]{:S(2)}, u32[]{:S(2)}) %collective-permute-start.2) | collective-permute-done | bytes 331808 | tf_op jit(solution)/shard_map/ppermute | solution.py:428
  170.9 20.3 %all_to_all.25.got_ref = bf16[16,96,128]{2,1,0:T(8,128)(2,1)S(1)} all-to-all(bf16[16,96,128]{2,1,0:T(8,128)(2,1)S(1)} %add_z.1), channel_id=1, replica_groups={{0,2,4,6,8,10,12,14,16,18,20,22,24,26,28,30},{1,3,5,7,9,11,13,15,17,19,..., dimensions={0} | all-to-all | bytes 786432 | tf_op jit(solution)/shard_map/all_to_all | solution.py:422
  191.2 0.8 add_frames.1
  192.0 4.8 %all-to-all-start.4 = ((f32[4,96,128]{2,1,0:T(8,128)}), f32[4,96,128]{2,1,0:T(8,128)S(1)}, u32[]{:S(2)}, u32[]{:S(2)}) async-start(f32[4,96,128]{2,1,0:T(8,128)} %add_frames.1), calls=%async_computation.4 | async-start | bytes 393216 | tf_op jit(solution)/shard_map/all_to_all | solution.py:422
  196.8 2.7 %slice_bitcast_fusion = (bf16[1,1,256,1152]{3,2,1,0:T(8,128)(2,1)}, bf16[1,1,256,1152]{3,2,1,0:T(8,128)(2,1)}, bf16[1,1,256,1152]{3,2,1,0:T(8,128)(2,1)}) fusion(bf16[32,3,8,1152]{3,2,1,0:T(8,128)(2,1)} %all-to-all-done.1), kind=kLoop, calls=%fused_computation.32 | loop fusion | bytes 3538944 | tf_op jit(solution)/shard_map/reshape;squeeze | solution.py:454
  199.4 2.2 %all-to-all-done.4.got_ref = f32[4,96,128]{2,1,0:T(8,128)S(1)} async-done(((f32[4,96,128]{2,1,0:T(8,128)}), f32[4,96,128]{2,1,0:T(8,128)S(1)}, u32[]{:S(2)}, u32[]{:S(2)}) %all-to-all-start.4) | async-done | bytes 196640 | tf_op jit(solution)/shard_map/all_to_all | solution.py:422
  201.6 0.7 assemble.1
  (11 shorter events, 0.6 us)
Async XLA Ops:
  10.3 74.4 %all-to-all-start = ((bf16[32,4,8,1152]{3,2,1,0:T(8,128)(2,1)}), bf16[32,4,8,1152]{3,2,1,0:T(8,128)(2,1)S(1)}, u32[]{:S(2)}, u32[]{:S(2)}) async-start(bf16[32,4,8,1152]{3,2,1,0:T(8,128)(2,1)} %pack.1), calls=%async_computation | async-start | bytes 4718592 | tf_op jit(solution)/shard_map/all_to_all | solution.py:422
  19.6 87.7 %all-gather.4.cloned.1.call-start = ((), (), s32[]{:S(2)}) async-start(), calls=%async_computation.5 | async-start | bytes 3041280 | tf_op jit(solution)/shard_map/all_gather | solution.py:432
  84.7 12.0 %copy-start = (bf16[32,4,8,1152]{3,2,1,0:T(8,128)(2,1)}, bf16[32,4,8,1152]{3,2,1,0:T(8,128)(2,1)S(1)}, u32[]{:S(2)}) copy-start(bf16[32,4,8,1152]{3,2,1,0:T(8,128)(2,1)S(1)} %all-to-all-done.got_ref) | copy-start | bytes 7077892
  89.4 4.4 %collective-permute-start = (bf16[256,1792]{1,0:T(8,128)(2,1)S(1)}, bf16[256,1792]{1,0:T(8,128)(2,1)S(1)}, u32[]{:S(2)}, u32[]{:S(2)}) collective-permute-start(bf16[256,1792]{1,0:T(8,128)(2,1)S(1)} %get-tuple-element.15), channel_id=1, source_target_pairs={{0,1},{1,0},{2,3},{3,2},{4,5},{5,4},{6,7},{7,6},{8,9},{9,8},{10,11... | collective-permute-start | bytes 2752520 | tf_op jit(solution)/shard_map/ppermute | solution.py:438
  96.7 22.3 %all-to-all-start.2 = ((bf16[4,144,1152]{2,1,0:T(8,128)(2,1)}), bf16[4,144,1152]{2,1,0:T(8,128)(2,1)S(1)}, u32[]{:S(2)}, u32[]{:S(2)}) async-start(bf16[4,144,1152]{2,1,0:T(8,128)(2,1)} %get-tuple-element.17), calls=%async_computation.2 | async-start | bytes 2654208 | tf_op jit(solution)/shard_map/all_to_all | solution.py:422
  119.0 51.9 %all-to-all-start.1 = ((bf16[32,3,8,1152]{3,2,1,0:T(8,128)(2,1)}), bf16[32,3,8,1152]{3,2,1,0:T(8,128)(2,1)}, u32[]{:S(2)}, u32[]{:S(2)}) async-start(bf16[32,3,8,1152]{3,2,1,0:T(8,128)(2,1)} %attention_gradients.1), calls=%async_computation.1 | async-start | bytes 3538944 | tf_op jit(solution)/shard_map/all_to_all | solution.py:422
  125.1 21.4 %collective-permute-start.1 = (bf16[144,1152]{1,0:T(8,128)(2,1)S(1)}, bf16[144,1152]{1,0:T(8,128)(2,1)S(1)}, u32[]{:S(2)}, u32[]{:S(2)}) collective-permute-start(bf16[144,1152]{1,0:T(8,128)(2,1)S(1)} %add_x.1), channel_id=1, source_target_pairs={{0,128},{32,160},{64,192},{96,224},{128,0},{160,32},{192,64},{224,... | collective-permute-start | bytes 995336 | tf_op jit(solution)/shard_map/ppermute | solution.py:428
  146.6 24.1 %collective-permute-start.2 = (bf16[144,1152]{1,0:T(8,128)(2,1)S(1)}, bf16[144,1152]{1,0:T(8,128)(2,1)S(1)}, u32[]{:S(2)}, u32[]{:S(2)}) collective-permute-start(bf16[144,1152]{1,0:T(8,128)(2,1)S(1)} %add_convert_fusion.a_ref), channel_id=1, source_target_pairs={{0,384},{32,416},{64,448},{96,480},{128,256},{160,288},{192,320},{... | collective-permute-start | bytes 995336 | tf_op jit(solution)/shard_map/ppermute | solution.py:428
  192.0 9.7 %all-to-all-start.4 = ((f32[4,96,128]{2,1,0:T(8,128)}), f32[4,96,128]{2,1,0:T(8,128)S(1)}, u32[]{:S(2)}, u32[]{:S(2)}) async-start(f32[4,96,128]{2,1,0:T(8,128)} %add_frames.1), calls=%async_computation.4 | async-start | bytes 393216 | tf_op jit(solution)/shard_map/all_to_all | solution.py:422
Sparse Core Ops, SparseCore 0:
  22.6 84.6 all-gather.3
